TPU v7x, 128 devices: a whole 4x4x4 slice. The times are simulated.
128 devices in a mesh: row: 16 (over x, z), col: 8 (over y, core).
Axes of the slice: x: 4, y: 4, z: 4, core: 2. Of those that a mesh axis runs over, the one named last changes fastest.
Arguments:
- roughness: float32 [8192, 8192], P('row', 'col'), may hold values from -6 to 6
- transfer_real: float32 [8192, 8192], P(('row', 'col')), may hold values from -6 to 6
- transfer_imag: float32 [8192, 8192], P(('row', 'col')), may hold values from -6 to 6
- station_cells: int32 [2, 65536], P(None, ('row', 'col')), may hold values from 0 to 8191, as said below
- station_weights: float32 [4, 65536], P(None, ('row', 'col')), may hold values from 0.1 to 1
- station_means: float32 [65536], P(('row', 'col')), may hold values from -6 to 6
- station_counts: int32 [128], P(('row', 'col')), may hold values from 64 to 512, as said below
Outputs:
- gradient: float32 [8192, 8192], P('row', 'col')
- misfit: float32 [65536], P(('row', 'col'))
Inputs may be any that keep to these rules, and one draw needn't show every extreme that they name: With t = s // 512, the cell (station_cells[0, s], station_cells[1, s]) lies in tile t: its first index in [(t // 8) * 512, (t // 8 + 1) * 512), its second in [(t mod 8) * 1024, (t mod 8 + 1) * 1024), with 8 the number of tiles along the second dimension. `station_counts`: some tile holds exactly 512 live stations.
All inputs are finite; a program needn't handle non-finite values.
Results may differ from a plain program's by a relative error of at most 0.000098.
Values sent between devices are 32-bit elements; how exact they have to be, the bound alone decides.
No kernel may reach another device: no remote copies, remote signals or barrier semaphores. Data moves between devices by JAX's collectives and lax.ppermute only.
A program may use at most 128 MiB of HBM per device.

v0:
```python
import math

import jax
import jax.numpy as jnp
from jax import lax
from jax.sharding import PartitionSpec as P

HIGHEST = lax.Precision.HIGHEST


def passed_along(array, axis, by):
    size = lax.axis_size(axis)
    return lax.ppermute(array, axis, [(i, (i + by) % size) for i in range(size)])


def angle_table(left, right, modulus):
    product = (
        jnp.arange(left, dtype=jnp.int32)[:, None]
        * jnp.arange(right, dtype=jnp.int32)[None, :]
        % modulus
    )
    angles = product.astype(jnp.float32) * (2.0 * math.pi / modulus)
    return (jnp.cos(angles), jnp.sin(angles))


def complex_contract(left_part, table_part, out_part, stacked, cos_tab, sin_tab, sign):
    table = jnp.stack([jnp.stack([cos_tab, sign * sin_tab]), jnp.stack([-sign * sin_tab, cos_tab])])
    return jnp.einsum(
        "c" + left_part + ",cd" + table_part + "->d" + out_part, stacked, table, precision=HIGHEST
    )


def real_in_contract(left_part, table_part, out_part, values, cos_tab, sin_tab, sign):
    table = jnp.stack([cos_tab, sign * sin_tab])
    return jnp.einsum(
        left_part + ",d" + table_part + "->d" + out_part, values, table, precision=HIGHEST
    )


def real_out_contract(left_part, table_part, out_part, stacked, cos_tab, sin_tab, sign):
    table = jnp.stack([cos_tab, -sign * sin_tab])
    return jnp.einsum(
        "c" + left_part + ",c" + table_part + "->" + out_part, stacked, table, precision=HIGHEST
    )


def twist(stacked, length, sign):
    tw_cos, tw_sin = angle_table(128, length // 128, length)
    real_in = stacked[0]
    imag_in = stacked[1]
    return jnp.stack(
        [real_in * tw_cos - sign * imag_in * tw_sin, imag_in * tw_cos + sign * real_in * tw_sin]
    )


def forward_rows(strips):
    block_width, length = strips.shape
    short_len = length // 128
    big_cos, big_sin = angle_table(128, 128, 128)
    small_cos, small_sin = angle_table(short_len, short_len, short_len)
    shaped = strips.reshape(block_width, 128, short_len)
    middle = real_in_contract("rmn", "mp", "rpn", shaped, big_cos, big_sin, -1.0)
    middle = twist(middle, length, -1.0)
    result = complex_contract("rpn", "nq", "qpr", middle, small_cos, small_sin, -1.0)
    pieces = length // block_width
    return result.reshape(2, pieces, block_width * block_width)


def forward_columns(stacked, x_width):
    pieces = stacked.shape[1]
    length = pieces * x_width
    k_width = stacked.shape[2] // x_width
    short_len = length // 128
    group = x_width // short_len
    big_cos, big_sin = angle_table(128, 128, 128)
    small_cos, small_sin = angle_table(short_len, short_len, short_len)
    big_cos = big_cos.reshape(pieces, group, 128)
    big_sin = big_sin.reshape(pieces, group, 128)
    shaped = stacked.reshape(2, pieces, k_width, group, short_len)
    middle = complex_contract("sbtn", "stp", "bpn", shaped, big_cos, big_sin, -1.0)
    middle = twist(middle, length, -1.0)
    result = complex_contract("bpn", "nq", "bqp", middle, small_cos, small_sin, -1.0)
    return result.reshape(2, k_width, length)


def inverse_columns(stacked, x_width):
    k_width, length = (stacked.shape[1], stacked.shape[2])
    short_len = length // 128
    big_cos, big_sin = angle_table(128, 128, 128)
    small_cos, small_sin = angle_table(short_len, short_len, short_len)
    shaped = stacked.reshape(2, k_width, 128, short_len)
    middle = complex_contract("bmn", "mp", "bpn", shaped, big_cos, big_sin, 1.0)
    middle = twist(middle, length, 1.0)
    split = 128 // x_width
    middle = middle.reshape(2, k_width, split, x_width, short_len)
    result = complex_contract("bhkn", "nq", "qhbk", middle, small_cos, small_sin, 1.0)
    pieces = length // x_width
    return result.reshape(2, pieces, k_width * x_width)


def inverse_rows(stacked, block_width):
    pieces = stacked.shape[1]
    length = pieces * block_width
    short_len = length // 128
    group = block_width // short_len
    big_cos, big_sin = angle_table(128, 128, 128)
    small_cos, small_sin = angle_table(short_len, short_len, short_len)
    big_cos = big_cos.reshape(pieces, group, 128)
    big_sin = big_sin.reshape(pieces, group, 128)
    shaped = stacked.reshape(2, pieces, group, short_len, block_width)
    middle = complex_contract("stnb", "stp", "bpn", shaped, big_cos, big_sin, 1.0)
    middle = twist(middle, length, 1.0)
    result = real_out_contract("bpn", "nq", "bqp", middle, small_cos, small_sin, 1.0)
    return result.reshape(block_width, length) * (1.0 / (length * length))


def respond(tiled, transfer_real, transfer_imag, sign):
    strips = lax.all_to_all(tiled, "col", split_axis=0, concat_axis=1, tiled=True)
    block_width, length = strips.shape
    rows_done = forward_rows(strips)
    moved = lax.all_to_all(rows_done, ("row", "col"), split_axis=1, concat_axis=1, tiled=True)
    spectrum = forward_columns(moved, block_width)
    signed_imag = sign * transfer_imag
    product = jnp.stack(
        [
            spectrum[0] * transfer_real - spectrum[1] * signed_imag,
            spectrum[0] * signed_imag + spectrum[1] * transfer_real,
        ]
    )
    returned = inverse_columns(product, block_width)
    home = lax.all_to_all(returned, ("row", "col"), split_axis=1, concat_axis=1, tiled=True)
    strips_out = inverse_rows(home, block_width)
    return lax.all_to_all(strips_out, "col", split_axis=1, concat_axis=0, tiled=True)


def local(
    roughness,
    transfer_real,
    transfer_imag,
    station_cells,
    station_weights,
    station_means,
    station_counts,
):
    response = respond(roughness, transfer_real, transfer_imag, 1.0)
    tile_rows, tile_cols = response.shape
    below = passed_along(response[:1], "row", -1)
    extended = jnp.concatenate([response, below], axis=0)
    beside = passed_along(extended[:, :1], "col", -1)
    extended = jnp.concatenate([extended, beside], axis=1)
    stride = tile_cols + 1
    local_rows = station_cells[0] - lax.axis_index("row") * tile_rows
    local_cols = station_cells[1] - lax.axis_index("col") * tile_cols
    corner_base = local_rows * stride + local_cols
    offsets = [0, 1, stride, stride + 1]
    flat_map = extended.reshape(-1)
    interp = jnp.zeros(corner_base.shape, jnp.float32)
    for which in range(4):
        interp = interp + station_weights[which] * flat_map[corner_base + offsets[which]]
    slot_count = station_means.shape[0]
    live = jnp.arange(slot_count, dtype=jnp.int32) < station_counts[0]
    misfit = jnp.where(live, interp - station_means, jnp.float32(0.0))
    all_index = jnp.concatenate([corner_base + offsets[which] for which in range(4)])
    all_values = jnp.concatenate([station_weights[which] * misfit for which in range(4)])
    forcing = jnp.zeros(((tile_rows + 1) * stride,), jnp.float32).at[all_index].add(all_values)
    forcing = forcing.reshape(tile_rows + 1, stride)
    from_left = passed_along(forcing[:, tile_cols:], "col", 1)
    folded_map = forcing[:, :tile_cols].at[:, 0:1].add(from_left)
    from_above = passed_along(folded_map[tile_rows:], "row", 1)
    forcing_tile = folded_map[:tile_rows].at[0:1].add(from_above)
    side = tile_cols * lax.axis_size("col")
    slots_all = slot_count * lax.axis_size("row") * lax.axis_size("col")
    scale = math.sqrt(side * side / slots_all)
    gradient = respond(forcing_tile, transfer_real, transfer_imag, -1.0) * scale
    return (gradient, misfit)


def solution(mesh):
    in_specs = (
        P("row", "col"),
        P(("row", "col"), None),
        P(("row", "col"), None),
        P(None, ("row", "col")),
        P(None, ("row", "col")),
        P(("row", "col")),
        P(("row", "col")),
    )
    out_specs = (P("row", "col"), P(("row", "col")))
    return jax.shard_map(local, mesh=mesh, in_specs=in_specs, out_specs=out_specs, check_vma=False)
```

profile of v0, /device:TPU:1, one launch (start us, length us, event | category | flops | bytes accessed | tf_op | source)
XLA Modules:
  0.0 726.4 jit_solution(10603240892155566698)
XLA Ops:
  0.6 6.0 all-to-all-start
  7.4 25.5 %all-to-all-done = f32[8,64,1024]{2,1,0:T(8,128)S(1)} async-done(((f32[8,64,1024]{2,1,0:T(8,128)}), f32[8,64,1024]{2,1,0:T(8,128)S(1)}, u32[]{:S(2)}, u32[]{:S(2)}) %all-to-all-start) | async-done | bytes 2097184 | tf_op jit(solution)/shard_map/all_to_all | solution.py:118
  39.6 8.6 %fusion.48 = f32[2,64,128,64]{2,3,1,0:T(8,128)S(1)} fusion(f32[64,128,64]{2,1,0:T(8,128)} %reshape.733, f32[1,128,128]{2,1,0:T(8,128)S(1)} %get-tuple-element.82, f32[1,128,128]{2,1,0:T(8,128)S(1)} %get-tuple-element.81), kind=kOutput, calls=%fused_computation.62 | convolution fusion | flops 1610645504 | bytes 6422528 | tf_op jit(solution)/shard_map/rmn,dmp->drpn/dot_general | solution.py:35
  54.6 7.0 copy.118
  61.7 8.1 %reshape.734 = f32[2,128,4096]{2,1,0:T(8,128)} reshape(f32[2,64,128,64]{3,2,1,0:T(8,128)} %copy.118) | data formatting | bytes 8388608 | tf_op jit(solution)/shard_map/reshape | solution.py:66
  69.8 7.4 %copy.119 = f32[2,128,4096]{2,0,1:T(2,128)} copy(f32[2,128,4096]{2,1,0:T(8,128)} %reshape.734) | data formatting | bytes 8388608 | tf_op jit(solution)/shard_map/reshape | solution.py:66
  77.2 9.3 %all-to-all-start.1 = ((f32[2,128,4096]{2,0,1:T(2,128)}), f32[2,128,4096]{2,0,1:T(2,128)}, u32[]{:S(2)}, u32[]{:S(2)}) async-start(f32[2,128,4096]{2,0,1:T(2,128)} %copy.119), calls=%async_computation.1 | async-start | bytes 8388608 | tf_op jit(solution)/shard_map/all_to_all | solution.py:121
  87.5 51.5 %all-to-all-done.1 = f32[2,128,4096]{2,0,1:T(2,128)} async-done(((f32[2,128,4096]{2,0,1:T(2,128)}), f32[2,128,4096]{2,0,1:T(2,128)}, u32[]{:S(2)}, u32[]{:S(2)}) %all-to-all-start.1) | async-done | bytes 4194336 | tf_op jit(solution)/shard_map/all_to_all | solution.py:121
  139.1 7.3 %copy.120 = f32[2,128,4096]{1,2,0:T(8,128)} copy(f32[2,128,4096]{2,0,1:T(2,128)} %all-to-all-done.1) | data formatting | bytes 8388608 | tf_op jit(solution)/shard_map/all_to_all | solution.py:121
  146.4 6.2 fusion.54
  194.0 14.3 %fusion.47 = f32[2,64,2,64,64]{4,1,2,3,0:T(8,128)S(1)} fusion(f32[1,64,2,64,64]{4,3,0,2,1:T(8,128)} %bitcast.318, f32[1,64,2,64,64]{4,3,0,2,1:T(8,128)} %bitcast.316, f32[1,2,64,64]{2,3,1,0:T(8,128)S(1)} %get-tuple-element.67, f32[1,2,64,64]{2,3,1,0:T(8,128)S(1)} %get-tuple-element.60), kind=kOutput, calls=%fused_computation.60 | convolution fusion | flops 1611677696 | bytes 8454144 | tf_op jit(solution)/shard_map/cbhkn,cdnq->dqhbk/dot_general | solution.py:28
  208.4 8.1 %copy.201 = f32[2,64,2,64,64]{4,3,0,2,1:T(8,128)} copy(f32[2,64,2,64,64]{4,1,2,3,0:T(8,128)S(1)} %fusion.47) | data formatting | bytes 8388608 | tf_op jit(solution)/shard_map/reshape | solution.py:98
  216.5 8.5 %reshape.823 = f32[2,128,4096]{2,0,1:T(2,128)} reshape(f32[2,64,2,64,64]{4,3,0,2,1:T(8,128)} %copy.201) | data formatting | bytes 8388608 | tf_op jit(solution)/shard_map/reshape | solution.py:98
  225.0 58.9 %all_to_all.78 = f32[2,128,4096]{2,0,1:T(2,128)} all-to-all(f32[2,128,4096]{2,0,1:T(2,128)} %reshape.823), channel_id=1, replica_groups=mesh['row'=16,'col'=8] {'row','col'}, dimensions={1} | all-to-all | bytes 8388608 | tf_op jit(solution)/shard_map/all_to_all | solution.py:131
  283.9 7.3 %copy.131 = f32[2,128,4096]{1,2,0:T(8,128)} copy(f32[2,128,4096]{2,0,1:T(2,128)} %all_to_all.78) | data formatting | bytes 8388608 | tf_op jit(solution)/shard_map/all_to_all | solution.py:131
  291.2 8.8 %fusion.60 = f32[2,64,128,64]{2,3,1,0:T(8,128)S(1)} fusion(f32[2,128,64,64,1]{1,3,2,0,4:T(8,128)} %bitcast.311, f32[1,2,128,1,128]{4,2,1,3,0:T(8,128)S(1)} %get-tuple-element.59, f32[1,2,128,1,128]{4,2,1,3,0:T(8,128)S(1)} %get-tuple-element.54), kind=kOutput, calls=%fused_computation.66 | convolution fusion | flops 3221291008 | bytes 8650752 | tf_op jit(solution)/shard_map/cstnb,cdstp->dbpn/dot_general | solution.py:28
  314.5 25.7 %all-to-all-done.3 = f32[64,8,1024]{2,0,1:T(8,128)S(1)} async-done(((f32[64,8,1024]{2,0,1:T(8,128)}), f32[64,8,1024]{2,0,1:T(8,128)S(1)}, u32[]{:S(2)}, u32[]{:S(2)}) %all-to-all-start.3) | async-done | bytes 2097184 | tf_op jit(solution)/shard_map/all_to_all | solution.py:133
  366.4 12.7 %scatter_custom_fusion = f32[525825]{0:T(1024)} fusion(s32[2048]{0:T(1024)S(1)} %bitcast.335, f32[2048]{0:T(1024)S(1)} %pad_maximum_fusion.18, f32[]{:T(128)} %constant.192.clone.1), kind=kCustom, calls=%fused_computation.106 | custom fusion | flops 2048 | bytes 2103304 | tf_op jit(solution)/shard_map/scatter-add | solution.py:165
  396.9 33.3 %all_to_all.79 = f32[8,64,1024]{2,1,0:T(8,128)S(1)} all-to-all(f32[8,64,1024]{2,1,0:T(8,128)S(1)} %bitcast.320), channel_id=1, replica_groups=mesh['row'=16,'col'=8] {'col'}, dimensions={0} | all-to-all | bytes 4194304 | tf_op jit(solution)/shard_map/all_to_all | solution.py:118
  433.9 8.6 %fusion.63 = f32[2,64,128,64]{2,3,1,0:T(8,128)S(1)} fusion(f32[64,128,64]{2,1,0:T(8,128)} %reshape.740, f32[1,128,128]{2,1,0:T(8,128)S(1)} %get-tuple-element.82, f32[1,128,128]{2,1,0:T(8,128)S(1)} %get-tuple-element.81), kind=kOutput, calls=%fused_computation.67 | convolution fusion | flops 1610645504 | bytes 6422528 | tf_op jit(solution)/shard_map/rmn,dmp->drpn/dot_general | solution.py:35
  448.9 7.0 copy.140
  456.0 8.0 %reshape.741 = f32[2,128,4096]{2,1,0:T(8,128)} reshape(f32[2,64,128,64]{3,2,1,0:T(8,128)} %copy.140) | data formatting | bytes 8388608 | tf_op jit(solution)/shard_map/reshape | solution.py:66
  469.3 57.7 %all_to_all.80 = f32[2,128,4096]{2,0,1:T(2,128)} all-to-all(f32[2,128,4096]{2,0,1:T(2,128)S(1)} %copy.141), channel_id=1, replica_groups=mesh['row'=16,'col'=8] {'row','col'}, dimensions={1} | all-to-all | bytes 8388608 | tf_op jit(solution)/shard_map/all_to_all | solution.py:121
  527.0 7.3 %copy.142 = f32[2,128,4096]{1,2,0:T(8,128)} copy(f32[2,128,4096]{2,0,1:T(2,128)} %all_to_all.80) | data formatting | bytes 8388608 | tf_op jit(solution)/shard_map/all_to_all | solution.py:121
  534.4 6.0 fusion.69
  580.5 14.7 %fusion.46 = f32[2,64,2,64,64]{4,1,2,3,0:T(8,128)S(1)} fusion(f32[1,64,2,64,64]{4,3,0,2,1:T(8,128)} %bitcast.317, f32[1,64,2,64,64]{4,3,0,2,1:T(8,128)} %bitcast.315, f32[1,2,64,64]{2,3,1,0:T(8,128)S(1)} %copy-done.9, f32[1,2,64,64]{2,3,1,0:T(8,128)S(1)} %copy-done.7), kind=kOutput, calls=%fused_computation.59 | convolution fusion | flops 1611677696 | bytes 8454144 | tf_op jit(solution)/shard_map/cbhkn,cdnq->dqhbk/dot_general | solution.py:28
  595.3 8.1 %copy.208 = f32[2,64,2,64,64]{4,3,0,2,1:T(8,128)} copy(f32[2,64,2,64,64]{4,1,2,3,0:T(8,128)S(1)} %fusion.46) | data formatting | bytes 8388608 | tf_op jit(solution)/shard_map/reshape | solution.py:98
  603.4 8.5 %reshape.824 = f32[2,128,4096]{2,0,1:T(2,128)} reshape(f32[2,64,2,64,64]{4,3,0,2,1:T(8,128)} %copy.208) | data formatting | bytes 8388608 | tf_op jit(solution)/shard_map/reshape | solution.py:98
  611.9 58.9 %all_to_all.81 = f32[2,128,4096]{2,0,1:T(2,128)} all-to-all(f32[2,128,4096]{2,0,1:T(2,128)} %reshape.824), channel_id=1, replica_groups=mesh['row'=16,'col'=8] {'row','col'}, dimensions={1} | all-to-all | bytes 8388608 | tf_op jit(solution)/shard_map/all_to_all | solution.py:131
  670.8 7.3 %copy.153 = f32[2,128,4096]{1,2,0:T(8,128)} copy(f32[2,128,4096]{2,0,1:T(2,128)} %all_to_all.81) | data formatting | bytes 8388608 | tf_op jit(solution)/shard_map/all_to_all | solution.py:131
  678.1 8.8 %fusion.75 = f32[2,64,128,64]{2,3,1,0:T(8,128)S(1)} fusion(f32[2,128,64,64,1]{1,3,2,0,4:T(8,128)} %bitcast.310, f32[1,2,128,1,128]{4,2,1,3,0:T(8,128)S(1)} %get-tuple-element.59, f32[1,2,128,1,128]{4,2,1,3,0:T(8,128)S(1)} %get-tuple-element.54), kind=kOutput, calls=%fused_computation.71 | convolution fusion | flops 3221291008 | bytes 8650752 | tf_op jit(solution)/shard_map/cstnb,cdstp->dbpn/dot_general | solution.py:28
  694.5 30.2 %all_to_all.82 = f32[64,8,1024]{2,0,1:T(8,128)S(1)} all-to-all(f32[64,8,1024]{2,0,1:T(8,128)S(1)} %copy.158), channel_id=1, replica_groups=mesh['row'=16,'col'=8] {'col'}, dimensions={1} | all-to-all | bytes 4194304 | tf_op jit(solution)/shard_map/all_to_all | solution.py:133
  (130 shorter events, 178.6 us)
Async XLA Ops:
  0.6 32.3 %all-to-all-start = ((f32[8,64,1024]{2,1,0:T(8,128)}), f32[8,64,1024]{2,1,0:T(8,128)S(1)}, u32[]{:S(2)}, u32[]{:S(2)}) async-start(f32[8,64,1024]{2,1,0:T(8,128)} %bitcast.326), calls=%async_computation | async-start | bytes 4194304 | tf_op jit(solution)/shard_map/all_to_all | solution.py:118
  6.8 294.2 %copy-start.10 = (f32[1,64,64]{1,2,0:T(8,128)}, f32[1,64,64]{1,2,0:T(8,128)S(1)}, u32[]{:S(2)}) copy-start(f32[1,64,64]{1,2,0:T(8,128)S(1)} %fusion.143) | copy-start | bytes 49156
  7.1 293.9 %copy-start.12 = (f32[1,64,64]{1,2,0:T(8,128)}, f32[1,64,64]{1,2,0:T(8,128)S(1)}, u32[]{:S(2)}) copy-start(f32[1,64,64]{1,2,0:T(8,128)S(1)} %get-tuple-element.85) | copy-start | bytes 49156
  7.4 186.6 %copy-start.6 = (f32[1,2,64,64]{2,3,1,0:T(8,128)}, f32[1,2,64,64]{2,3,1,0:T(8,128)S(1)}, u32[]{:S(2)}) copy-start(f32[1,2,64,64]{2,3,1,0:T(8,128)S(1)} %get-tuple-element.60) | copy-start | bytes 98308
  7.4 186.6 %copy-start.8 = (f32[1,2,64,64]{2,3,1,0:T(8,128)}, f32[1,2,64,64]{2,3,1,0:T(8,128)S(1)}, u32[]{:S(2)}) copy-start(f32[1,2,64,64]{2,3,1,0:T(8,128)S(1)} %get-tuple-element.67) | copy-start | bytes 98308
  32.9 1.3 copy-start
  77.2 61.8 %all-to-all-start.1 = ((f32[2,128,4096]{2,0,1:T(2,128)}), f32[2,128,4096]{2,0,1:T(2,128)}, u32[]{:S(2)}, u32[]{:S(2)}) async-start(f32[2,128,4096]{2,0,1:T(2,128)} %copy.119), calls=%async_computation.1 | async-start | bytes 8388608 | tf_op jit(solution)/shard_map/all_to_all | solution.py:121
  157.4 1.6 copy-start.2
  157.4 2.2 copy-start.4
  176.0 4.3 copy-start.1
  308.9 4.9 copy-start.17
  308.9 5.0 copy-start.15
  308.9 31.3 %all-to-all-start.3 = ((f32[64,8,1024]{2,0,1:T(8,128)}), f32[64,8,1024]{2,0,1:T(8,128)S(1)}, u32[]{:S(2)}, u32[]{:S(2)}) async-start(f32[64,8,1024]{2,0,1:T(8,128)} %copy.136), calls=%async_computation.3 | async-start | bytes 4194304 | tf_op jit(solution)/shard_map/all_to_all | solution.py:133
  340.2 2.8 collective-permute-start
  343.0 6.0 collective-permute-start.1
  360.0 6.3 copy-start.16
  360.0 6.3 copy-start.18
  366.4 15.9 %copy-start.14 = (f32[512]{0:T(512)}, f32[512]{0:T(512)S(1)}, u32[]{:S(2)}) copy-start(f32[512]{0:T(512)S(1)} %get-tuple-element.27) | copy-start | bytes 6148
  382.3 3.4 collective-permute-start.2
  389.7 6.3 collective-permute-start.3
  545.2 1.6 copy-start.3
  545.2 2.2 copy-start.5
  577.8 2.7 copy-start.7
  577.8 2.7 copy-start.9
  686.9 1.0 copy-start.11
  686.9 1.0 copy-start.13
where the time goes:
time: 736 us; the launch traced here: 726 us
  blocking collectives  239 us (32%)
  local copies, waits for them, and re-layouts  199 us (27%)
  waiting for transfers between devices  113 us (15%)
  matrix products  109 us (15%)
  other arithmetic  40.2 us (5%)
  starting transfers between devices  24.1 us (3%)
    all_to_all x2, blocking collectives, respond(): lax.all_to_all(returned, ('row', 'col'), split_axis=1, concat_axis=1, til...  118 us
    dot_general x12, matrix products, complex_contract(): jnp.einsum('c' + left_part + ',cd' + table_part + '->d' + out_part, stack...  87.5 us
    all_to_all x1, blocking collectives, respond(): lax.all_to_all(rows_done, ('row', 'col'), split_axis=1, concat_axis=1, ti...  57.7 us
    all_to_all x1, waiting for transfers between devices, respond(): lax.all_to_all(rows_done, ('row', 'col'), split_axis=1, concat_axis=1, ti...  51.5 us
    all_to_all x1, blocking collectives, respond(): lax.all_to_all(tiled, 'col', split_axis=0, concat_axis=1, tiled=True)  33.3 us
    reshape x4, local copies, waits for them, and re-layouts, inverse_columns(): return result.reshape(2, pieces, k_width * x_width)  33.2 us
    all_to_all x1, blocking collectives, respond(): lax.all_to_all(strips_out, 'col', split_axis=1, concat_axis=0, tiled=True)  30.2 us
    another operation x8, local copies, waits for them, and re-layouts, respond(): jnp.stack([spectrum[0] * transfer_real - spectrum[1] * signed_imag, spect...  30.1 us
  transfers between devices with their start and end apart: 7, of which 7 were waited for; matrix products, arithmetic and copies ran while one was open for 1% of the time, Pallas kernels for 0%

commit v1 on v0

v1 whole, which is shorter than its diff:
```python
import functools
import math

import jax
import jax.numpy as jnp
import numpy as np
from jax import lax
from jax.experimental import pallas as pl
from jax.experimental.pallas import tpu as pltpu
from jax.sharding import PartitionSpec as P

F32 = jnp.float32
BF16 = jnp.bfloat16

N = 8192
LANES = 128
SHORT = 64
PAIRS = 17
ROWS = 2 * PAIRS
VMEM_LIMIT = 40 * 1024 * 1024


def split_np(table):
    hi = table.astype(np.float32).astype(jnp.bfloat16)
    lo = (table - hi.astype(np.float64)).astype(np.float32).astype(jnp.bfloat16)
    return np.stack([hi, lo])


def complex_table(length, copies, sign):
    index = np.arange(length)
    angles = 2.0 * np.pi * (index[:, None] * index[None, :] % length) / length
    cos = np.kron(np.eye(copies), np.cos(angles))
    sin = sign * np.kron(np.eye(copies), np.sin(angles))
    return np.block([[cos, -sin], [sin, cos]])


def twiddle_table(left, right, sign):
    angles = 2.0 * np.pi * (left[:, None] * right[None, :] % N) / N
    return np.stack([np.cos(angles), sign * np.sin(angles)]).astype(np.float32)


def split(x):
    hi = x.astype(BF16)
    lo = (x - hi.astype(F32)).astype(BF16)
    return hi, lo


def mm(a, b, dims):
    return lax.dot_general(a, b, (dims, ((), ())), preferred_element_type=F32)


NN = ((1,), (0,))
NT = ((1,), (1,))


def table_times(tab, data, dims):
    hi, lo = split(data)
    return mm(tab[0], hi, dims) + (mm(tab[1], hi, dims) + mm(tab[0], lo, dims))


def times_table(data, tab, dims):
    hi, lo = split(data)
    return mm(hi, tab[0], dims) + (mm(hi, tab[1], dims) + mm(lo, tab[0], dims))


RT = math.sqrt(0.5)


def cadd(a, b):
    return (a[0] + b[0], a[1] + b[1])


def csub(a, b):
    return (a[0] - b[0], a[1] - b[1])


def cmul(a, b):
    return (a[0] * b[0] - a[1] * b[1], a[0] * b[1] + a[1] * b[0])


def times_i(a, sign):
    return (-a[1], a[0]) if sign > 0 else (a[1], -a[0])


def turn(a, angle):
    c, s = math.cos(angle), math.sin(angle)
    return (a[0] * c - a[1] * s, a[0] * s + a[1] * c)


def dft4(x, sign):
    a, b = cadd(x[0], x[2]), csub(x[0], x[2])
    c, d = cadd(x[1], x[3]), times_i(csub(x[1], x[3]), sign)
    return [cadd(a, c), cadd(b, d), csub(a, c), csub(b, d)]


def eighth(a, sign):
    if sign > 0:
        return ((a[0] - a[1]) * RT, (a[0] + a[1]) * RT)
    return ((a[0] + a[1]) * RT, (a[1] - a[0]) * RT)


def dft8(x, sign):
    even = dft4(x[0::2], sign)
    odd = dft4(x[1::2], sign)
    odd[1] = eighth(odd[1], sign)
    odd[2] = times_i(odd[2], sign)
    odd[3] = times_i(eighth(odd[3], sign), sign)
    return [cadd(even[i], odd[i]) for i in range(4)] + [csub(even[i], odd[i]) for i in range(4)]


def real_dft8(x):
    a, b = x[0] + x[4], x[0] - x[4]
    c, d = x[2] + x[6], x[2] - x[6]
    e, f = x[1] + x[5], x[1] - x[5]
    g, h = x[3] + x[7], x[3] - x[7]
    even, odd = a + c, e + g
    u, v = (f - h) * RT, (f + h) * RT
    return [(even + odd, None), (b + u, -(d + v)), (a - c, g - e), (b - u, d - v), (even - odd, None)]


def real_fft64(x):
    first = [real_dft8([x[8 * u + v] for u in range(8)]) for v in range(8)]
    out = [None] * 33
    zero_part = real_dft8([first[v][0][0] for v in range(8)])
    for t in range(5):
        out[8 * t] = zero_part[t]
    for s in range(1, 4):
        turned = [first[0][s]] + [turn(first[v][s], -2 * math.pi * v * s / 64) for v in range(1, 8)]
        done = dft8(turned, -1)
        for t in range(8):
            p = s + 8 * t
            if p <= 32:
                out[p] = done[t]
            else:
                out[64 - p] = (done[t][0], -done[t][1])
    real = [first[v][4][0] for v in range(8)]
    turned = []
    for v in range(8):
        c, s = math.cos(2 * math.pi * v / 16), -math.sin(2 * math.pi * v / 16)
        turned.append((real[v] * c, real[v] * s))
    turned[0] = (real[0], jnp.zeros_like(real[0]))
    done = dft8(turned, -1)
    for t in range(4):
        out[4 + 8 * t] = done[t]
    return out


def real_of_inverse8(zero, four, one, two, three):
    a, b = zero + four, zero - four
    res = [None] * 8
    even_p, even_m = a + two[0], a - two[0]
    odd_p, odd_m = b - two[1], b + two[1]
    sum_r, dif_i = one[0] + three[0], one[1] - three[1]
    res[0], res[4] = even_p + sum_r, even_p - sum_r
    res[2], res[6] = even_m - dif_i, even_m + dif_i
    k1 = ((one[0] - three[0]) - (one[1] + three[1])) * RT
    k3 = ((three[0] - one[0]) - (one[1] + three[1])) * RT
    res[1], res[5] = odd_p + k1, odd_p - k1
    res[3], res[7] = odd_m + k3, odd_m - k3
    return res


def real_of_inverse64(v):
    zero = real_of_inverse8(v[0][0], v[32][0], v[8], v[16], v[24])
    parts = [v[4], v[12], v[20], v[28]]
    four = []
    quarter = dft4(parts, 1)
    turned = [parts[0], eighth(parts[1], 1), times_i(parts[2], 1), times_i(eighth(parts[3], 1), 1)]
    shifted = dft4(turned, 1)
    for m in range(8):
        value = quarter[m // 2] if m % 2 == 0 else shifted[m // 2]
        angle = 2 * math.pi * m / 16
        four.append(value[0] * math.cos(angle) - value[1] * math.sin(angle) if m else value[0])
    others = []
    for s in range(1, 4):
        x = []
        for t in range(8):
            p = s + 8 * t
            x.append(v[p] if p <= 32 else (v[64 - p][0], -v[64 - p][1]))
        done = dft8(x, 1)
        others.append([done[0]] + [turn(done[m], 2 * math.pi * m * s / 64) for m in range(1, 8)])
    out = [None] * 64
    for m in range(8):
        res = real_of_inverse8(zero[m], four[m], others[0][m], others[1][m], others[2][m])
        for u in range(8):
            out[8 * u + m] = res[u]
    return out


def rows_forward_kernel(has_carry, *refs):
    if has_carry:
        strip, carry, tab, tw, out, z = refs
    else:
        strip, tab, tw, out, z = refs

    def lines(t, _):
        x0 = pl.multiple_of(t * 8, 8)
        x = []
        for m in range(64):
            value = strip[m // 8, pl.ds(x0, 8), (m % 8) * LANES : (m % 8 + 1) * LANES]
            if has_carry:
                here = (lax.broadcasted_iota(jnp.int32, (8, LANES), 0) + x0) == 0
                value = value + jnp.where(here, carry[m : m + 1, :], 0.0)
            x.append(value)
        done = real_fft64(x)
        for p in range(33):
            re, im = done[p]
            c, s = tw[0, p : p + 1, :], tw[1, p : p + 1, :]
            if im is None:
                new_re, new_im = re * c, re * s
            else:
                new_re, new_im = re * c - im * s, re * s + im * c
            z[pl.ds(p * 64 + x0, 8), 0:LANES] = new_re
            z[pl.ds(p * 64 + x0, 8), LANES : 2 * LANES] = new_im
        return 0

    lax.fori_loop(0, 8, lines, 0)
    z[33 * 64 :, :] = jnp.zeros((64, 2 * LANES), F32)

    def pair(j, _):
        data = z[pl.ds(pl.multiple_of(j * 128, 128), 128), :]
        res = table_times(tab, data, NT)
        out[pl.ds(2 * j, 128, stride=ROWS), :] = res[:128]
        out[pl.ds(2 * j + 1, 128, stride=ROWS), :] = res[128:]
        return 0

    lax.fori_loop(0, PAIRS, pair, 0, unroll=True)


def columns_kernel(conj, moved, g_re, g_im, tab1, tab2, tab2i, tab1i, tw, twt, out):
    def pair(j, _):
        data = jnp.concatenate(
            [moved[pl.ds(2 * j, 128, stride=ROWS), :], moved[pl.ds(2 * j + 1, 128, stride=ROWS), :]], axis=0
        )
        y = table_times(tab1, data, NN)
        re, im = cmul((y[:128], y[128:]), (tw[0], tw[1]))
        spec = table_times(tab2, jnp.concatenate([re, im], axis=1), NT)
        gr = g_re[pl.ds(2 * j, 2)].reshape(128, LANES)
        gi = g_im[pl.ds(2 * j, 2)].reshape(128, LANES)
        if conj:
            gi = -gi
        re, im = cmul((spec[:128], spec[128:]), (gr, gi))
        w = table_times(tab2i, jnp.concatenate([re, im], axis=0), NN)
        re, im = cmul((w[:128], w[128:]), (twt[0], twt[1]))
        res = table_times(tab1i, jnp.concatenate([re, im], axis=1), NT)
        out[pl.ds(2 * j, 128, stride=ROWS), :] = res[:128]
        out[pl.ds(2 * j + 1, 128, stride=ROWS), :] = res[128:]
        return 0

    lax.fori_loop(0, PAIRS, pair, 0, unroll=True)


def rows_inverse_kernel(scale, home, tab, tw, out, v):
    def pair(j, _):
        re = home[pl.ds(2 * j, 128, stride=ROWS), :].T
        im = home[pl.ds(2 * j + 1, 128, stride=ROWS), :].T
        y = times_table(jnp.concatenate([re, im], axis=1), tab, NT)
        re, im = y[:, :LANES], y[:, LANES:]
        for half in range(2):
            p = 2 * j + half
            c, s = tw[0, pl.ds(p, 1), :] * scale, tw[1, pl.ds(p, 1), :] * scale
            a, b = re[half * 64 : half * 64 + 64], im[half * 64 : half * 64 + 64]
            rows = pl.ds(pl.multiple_of(j * 128 + half * 64, 64), 64)
            v[rows, 0:LANES] = a * c - b * s
            v[rows, LANES : 2 * LANES] = a * s + b * c
        return 0

    lax.fori_loop(0, PAIRS, pair, 0, unroll=True)

    def lines(t, _):
        x0 = pl.multiple_of(t * 8, 8)
        values = []
        for p in range(33):
            rows = pl.ds(p * 64 + x0, 8)
            values.append((v[rows, 0:LANES], v[rows, LANES : 2 * LANES]))
        done = real_of_inverse64(values)
        for m in range(64):
            out[m // 8, pl.ds(x0, 8), (m % 8) * LANES : (m % 8 + 1) * LANES] = done[m]
        return 0

    lax.fori_loop(0, 8, lines, 0)


def stations_kernel(r, edge, st, stt, force, spill, mis_out, r4, f4):
    lane64 = lax.broadcasted_iota(jnp.int32, (64, LANES), 1)
    row64 = lax.broadcasted_iota(jnp.int32, (64, LANES), 0)
    eye = lax.broadcasted_iota(jnp.int32, (128, 128), 0) == lax.broadcasted_iota(jnp.int32, (128, 128), 1)

    def shifted(t, _):
        after = lax.rem(t + 1, 8)
        own, down = [], []
        for m in range(9):
            a = r[t, :, m * LANES : (m + 1) * LANES] if m < 8 else r[after, :, 0:LANES]
            line = edge[pl.ds(t * 8 + m, 1), :] if m < 8 else edge[pl.ds(after * 8, 1), :]
            own.append(a)
            down.append(jnp.where(row64 == 63, line, pltpu.roll(a, 63, 0)))
        own_l = [pltpu.roll(a, LANES - 1, 1) for a in own]
        down_l = [pltpu.roll(a, LANES - 1, 1) for a in down]
        for m in range(8):
            rows = pl.ds(pl.multiple_of(t * 512 + m * 64, 64), 64)
            four = [
                own[m],
                jnp.where(lane64 == LANES - 1, own_l[m + 1], own_l[m]),
                down[m],
                jnp.where(lane64 == LANES - 1, down_l[m + 1], down_l[m]),
            ]
            for k in range(4):
                hi, lo = split(four[k])
                r4[0, rows, k * LANES : (k + 1) * LANES] = hi
                r4[1, rows, k * LANES : (k + 1) * LANES] = lo
        return 0

    lax.fori_loop(0, 8, shifted, 0)

    lane512 = lax.broadcasted_iota(jnp.int32, (512, LANES), 1).astype(F32)
    key_cols = lax.broadcasted_iota(jnp.int32, (512, 512), 1).astype(F32)
    key_rows = lax.broadcasted_iota(jnp.int32, (512, 512), 0).astype(F32)

    def tile(t, _):
        col = stt[t]
        key, low = col[:, 0:1], col[:, 1:2]
        pick = jnp.where(key_cols == key, 1.0, 0.0).astype(BF16)
        rows = pl.ds(pl.multiple_of(t * 512, 512), 512)
        got = mm(pick, r4[0, rows, :], NN) + mm(pick, r4[1, rows, :], NN)
        value = col[:, 2:3] * got[:, 0:LANES]
        for k in range(1, 4):
            value = value + col[:, 2 + k : 3 + k] * got[:, k * LANES : (k + 1) * LANES]
        here = lane512 == low
        interp = jnp.sum(jnp.where(here, value, 0.0), axis=1, keepdims=True)
        misfit = jnp.where(col[:, 7:8] > 0.5, interp - col[:, 6:7], 0.0)
        for i in range(4):
            part = jnp.where(eye, misfit[i * 128 : (i + 1) * 128], 0.0)
            mis_out[t, :, i * 128 : (i + 1) * 128] = jnp.sum(part, axis=0, keepdims=True)
        spread = jnp.where(here, misfit, 0.0)
        values = jnp.concatenate([spread * col[:, 2 + k : 3 + k] for k in range(4)], axis=1)
        hi, lo = split(values)
        back = jnp.where(key_rows == st[t, 0:1, :], 1.0, 0.0).astype(BF16)
        f4[rows, :] = mm(back, hi, NN) + mm(back, lo, NN)
        return 0

    lax.fori_loop(0, 8, tile, 0)

    def assemble(t, _):
        before = lax.rem(t + 7, 8)
        last = []
        for m in range(-1, 8):
            start = before * 512 + 448 if m < 0 else t * 512 + m * 64
            rows = pl.ds(pl.multiple_of(start, 64), 64)
            last.append([pltpu.roll(f4[rows, k * LANES : (k + 1) * LANES], 1, 1) for k in (1, 3)])
        for m in range(8):
            rows = pl.ds(pl.multiple_of(t * 512 + m * 64, 64), 64)
            same = f4[rows, 0:LANES] + jnp.where(lane64 == 0, last[m][0], last[m + 1][0])
            below = f4[rows, 2 * LANES : 3 * LANES] + jnp.where(lane64 == 0, last[m][1], last[m + 1][1])
            spill[pl.ds(t * 8 + m, 1), :] = below[63:64, :]
            force[t, :, m * LANES : (m + 1) * LANES] = same + jnp.where(row64 == 0, 0.0, pltpu.roll(below, 1, 0))
        return 0

    lax.fori_loop(0, 8, assemble, 0)


def mirror_kernel(t_re, t_im, m_re, m_im, rows_tab, lane_tab, g_re, g_im):
    lane = lax.broadcasted_iota(jnp.int32, (64, LANES), 1)
    g_re[0], g_im[0] = t_re[0], t_im[0]
    g_re[32], g_im[32] = t_re[32], t_im[32]
    g_re[33], g_im[33] = jnp.zeros((64, LANES), F32), jnp.zeros((64, LANES), F32)

    def one(p, _):
        both = jnp.concatenate([m_re[31 - p], m_im[31 - p]], axis=1)
        total = []
        for part in split(both):
            flipped = mm(rows_tab[...], part, NN).astype(BF16)
            total.append([mm(flipped[:, :LANES], lane_tab[...], NN), mm(flipped[:, LANES:], lane_tab[...], NN)])
        re, im = total[0][0] + total[1][0], total[0][1] + total[1][1]
        g_re[p] = t_re[p] + jnp.where(lane == 0, re[64:], re[:64])
        g_im[p] = t_im[p] - jnp.where(lane == 0, im[64:], im[:64])
        return 0

    lax.fori_loop(1, 32, one, 0)


def call(kernel, out_shape, scratch, *args, name, cost=None):
    single = isinstance(out_shape, jax.ShapeDtypeStruct)
    vmem = pl.BlockSpec(memory_space=pltpu.VMEM)
    return pl.pallas_call(
        kernel,
        out_shape=out_shape,
        in_specs=[vmem] * len(args),
        out_specs=vmem if single else [vmem] * len(out_shape),
        scratch_shapes=scratch,
        compiler_params=pltpu.CompilerParams(vmem_limit_bytes=VMEM_LIMIT),
        cost_estimate=cost,
        name=name,
    )(*args)


def cost(us):
    return pl.CostEstimate(flops=int(us * 1.0e9), bytes_accessed=4 * 1024 * 1024, transcendentals=0)


def shape(*dims, dtype=F32):
    return jax.ShapeDtypeStruct(dims, dtype)


def tables():
    n = np.arange(LANES)
    p = np.minimum(np.arange(ROWS), 32)
    x1 = np.arange(128) % 64
    fwd, inv = complex_table(128, 1, -1.0), complex_table(128, 1, 1.0)
    fwd2, inv2 = complex_table(64, 2, -1.0), complex_table(64, 2, 1.0)
    return {
        "fwd": split_np(fwd),
        "inv": split_np(inv),
        "fwd2": split_np(fwd2),
        "inv2": split_np(inv2),
        "row_fwd": twiddle_table(p, n, -1.0),
        "row_inv": twiddle_table(p, n, 1.0),
        "col_fwd": twiddle_table(n, x1, -1.0),
        "col_inv": twiddle_table(x1, n, 1.0),
    }


def rows_forward(strip, carry, tabs):
    args = [strip] + ([] if carry is None else [carry]) + [tabs["fwd"], tabs["row_fwd"]]
    return call(
        functools.partial(rows_forward_kernel, carry is not None),
        shape(128 * ROWS, LANES),
        [pltpu.VMEM((ROWS * 64, 2 * LANES), F32)],
        *args,
        name="rows_forward",
        cost=cost(6),
    )


def columns(moved, g_re, g_im, conj, tabs):
    return call(
        functools.partial(columns_kernel, conj),
        shape(128 * ROWS, LANES),
        [],
        moved,
        g_re,
        g_im,
        tabs["fwd"],
        tabs["fwd2"],
        tabs["inv2"],
        tabs["inv"],
        tabs["col_fwd"],
        tabs["col_inv"],
        name="columns",
        cost=cost(8),
    )


def rows_inverse(home, scale, tabs):
    return call(
        functools.partial(rows_inverse_kernel, scale),
        shape(8, 64, 1024),
        [pltpu.VMEM((ROWS * 64, 2 * LANES), F32)],
        home,
        tabs["inv"],
        tabs["row_inv"],
        name="rows_inverse",
        cost=cost(6),
    )


def stations(r, edge, st, stt):
    return call(
        stations_kernel,
        (shape(8, 64, 1024), shape(64, LANES), shape(8, 1, 512)),
        [pltpu.VMEM((2, 4096, 512), BF16), pltpu.VMEM((4096, 512), F32)],
        r,
        edge,
        st,
        stt,
        name="stations",
        cost=cost(15),
    )


def mirror(t_re, t_im, m_re, m_im):
    b = np.arange(64)
    rows = np.zeros((128, 64), np.float32)
    rows[b, 63 - b] = 1.0
    rows[64 + b, (64 - b) % 64] = 1.0
    a = np.arange(128)
    lanes = np.zeros((128, 128), np.float32)
    lanes[(128 - a) % 128, a] = 1.0
    return call(
        mirror_kernel,
        (shape(ROWS, 64, LANES), shape(ROWS, 64, LANES)),
        [],
        t_re,
        t_im,
        m_re,
        m_im,
        jnp.asarray(rows, BF16),
        jnp.asarray(lanes, BF16),
        name="mirror",
        cost=cost(6),
    )


BOTH = ("row", "col")


def swap(array):
    return lax.all_to_all(array, BOTH, split_axis=0, concat_axis=0, tiled=True)


def across(array):
    return lax.all_to_all(array, "col", split_axis=0, concat_axis=0, tiled=True)


def ring(array, by):
    return lax.ppermute(array, BOTH, [(i, (i + by) % 128) for i in range(128)])


def station_fields(cells, weights, means, counts):
    slots = means.shape[0]
    local_x = cells[0] - lax.axis_index("row") * 512
    local_y = cells[1] - lax.axis_index("col") * 1024
    live = jnp.arange(slots, dtype=jnp.int32) < counts[0]
    fields = jnp.stack(
        [local_x.astype(F32), local_y.astype(F32)]
        + [weights[k] for k in range(4)]
        + [means, live.astype(F32)]
    )
    gathered = lax.all_gather(fields, "col", axis=0, tiled=False)
    x = gathered[:, 0] - lax.axis_index("col").astype(F32) * 64.0
    y = gathered[:, 1]
    high = jnp.floor(y * (1.0 / 128.0))
    inside = (x >= 0.0) & (x < 64.0)
    key = jnp.where(inside, high * 64.0 + x, -1.0)
    live_here = jnp.where(inside, gathered[:, 7], 0.0)
    rest = [gathered[:, k] for k in range(2, 7)]
    return jnp.stack([key, y - high * 128.0] + rest + [live_here], axis=1)


def local(
    roughness,
    transfer_real,
    transfer_imag,
    station_cells,
    station_weights,
    station_means,
    station_counts,
):
    tabs = tables()
    t_re = transfer_real.reshape(64, 64, 128)
    t_im = transfer_imag.reshape(64, 64, 128)
    mirrored = [(i, 127 - i) for i in range(128)]
    m_re = lax.ppermute(t_re[33:], BOTH, mirrored)
    m_im = lax.ppermute(t_im[33:], BOTH, mirrored)
    st = station_fields(station_cells, station_weights, station_means, station_counts)
    stt = jnp.swapaxes(st, 1, 2)

    strip = across(roughness.reshape(8, 64, 1024))
    moved = swap(rows_forward(strip, None, tabs))
    g_re, g_im = mirror(t_re, t_im, m_re, m_im)
    home = swap(columns(moved, g_re, g_im, False, tabs))
    response = rows_inverse(home, 1.0 / (N * N), tabs)

    edge = ring(response[:, 0, :].reshape(64, 128), -1)
    force, spill, misfits = stations(response, edge, st, stt)
    carry = ring(spill, 1)
    misfit = lax.psum_scatter(misfits, "col", scatter_dimension=0, tiled=True).reshape(512)

    moved = swap(rows_forward(force, carry, tabs))
    home = swap(columns(moved, g_re, g_im, True, tabs))
    scale = math.sqrt(N * N / 65536.0) / (N * N)
    gradient = across(rows_inverse(home, scale, tabs)).reshape(512, 1024)
    return (gradient, misfit)


def solution(mesh):
    in_specs = (
        P("row", "col"),
        P(("row", "col"), None),
        P(("row", "col"), None),
        P(None, ("row", "col")),
        P(None, ("row", "col")),
        P(("row", "col")),
        P(("row", "col")),
    )
    out_specs = (P("row", "col"), P(("row", "col")))
    return jax.shard_map(local, mesh=mesh, in_specs=in_specs, out_specs=out_specs, check_vma=False)
```

time: 736 us -> 425 us (0.58)
  local copies, waits for them, and re-layouts: 199 us -> 42 us
  matrix products: 109 us -> 0 us
  Pallas kernels: 0 us -> 70.9 us
  blocking collectives: 239 us -> 197 us
  other arithmetic: 40.2 us -> 0.15 us
  waiting for transfers between devices: 113 us -> 77.4 us
    all_to_all x5 -> x3, blocking collectives: 239 us -> 123 us  [the longest x2 90.6 us: swap(): return lax.all_to_all(array, BOTH, split_axis=0, concat_axis=0, tiled=True)]
    dot_general x16 -> x0, matrix products: 109 us -> none  [the longest x12 87.5 us: complex_contract(): jnp.einsum('c' + left_part + ',cd' + table_part + '->d' + out_part, stack...]
    all_to_all x3, waiting for transfers between devices: 103 us -> 0.01 us  [the longest x2 0.01 us: swap(): return lax.all_to_all(array, BOTH, split_axis=0, concat_axis=0, tiled=True)]
    reshape x12 -> x0, local copies, waits for them, and re-layouts: 73.1 us -> none  [the longest x4 33.2 us: inverse_columns(): return result.reshape(2, pieces, k_width * x_width)]
    pallas_call x0 -> x8, Pallas kernels: none -> 70.9 us  [call(): pl.pallas_call(kernel, out_shape=out_shape, in_specs=[vmem] * len(args),...]
    ppermute x4, waiting for transfers between devices: 9.87 us -> 77.4 us  [the longest x1 47.2 us: local(): m_re = lax.ppermute(t_re[33:], BOTH, mirrored)]
    another operation x12 -> x2, local copies, waits for them, and re-layouts: 43.3 us -> 0.63 us  [the longest x1 0.6 us: station_fields(): return jnp.stack([key, y - high * 128.0] + rest + [live_here], axis=1)]
    unnamed x0 -> x1, blocking collectives: none -> 39.3 us
  transfers between devices with their start and end apart: 7 -> 7, of which waited for: 7 -> 4; matrix products, arithmetic and copies ran while one was open for 1% -> 1% of each run, Pallas kernels for 0% -> 2%
where the time goes in v1:
time: 425 us; the launch traced here: 419 us
  blocking collectives  197 us (46%)
  waiting for transfers between devices  77.4 us (18%)
  Pallas kernels  70.9 us (17%)
  local copies, waits for them, and re-layouts  42 us (10%)
  starting transfers between devices  29.5 us (7%)
    all_to_all x2, blocking collectives, swap(): return lax.all_to_all(array, BOTH, split_axis=0, concat_axis=0, tiled=True)  90.6 us
    pallas_call x8, Pallas kernels, call(): pl.pallas_call(kernel, out_shape=out_shape, in_specs=[vmem] * len(args),...  70.9 us
    ppermute x1, waiting for transfers between devices, local(): m_re = lax.ppermute(t_re[33:], BOTH, mirrored)  47.2 us
    unnamed x1, blocking collectives  39.3 us
    all_gather x1, blocking collectives, station_fields(): gathered = lax.all_gather(fields, 'col', axis=0, tiled=False)  34.8 us
    all_to_all x1, blocking collectives, across(): return lax.all_to_all(array, 'col', split_axis=0, concat_axis=0, tiled=True)  32.6 us
    ppermute x1, waiting for transfers between devices, local(): m_im = lax.ppermute(t_im[33:], BOTH, mirrored)  21.3 us
    unnamed x65, local copies, waits for them, and re-layouts  20.2 us
  transfers between devices with their start and end apart: 7, of which 4 were waited for; matrix products, arithmetic and copies ran while one was open for 1% of the time, Pallas kernels for 2%

profile of v1, /device:TPU:1, one launch (start us, length us, event | category | flops | bytes accessed | tf_op | source)
XLA Modules:
  0.0 419.4 jit_solution(1168195707092382713)
XLA Ops:
  0.7 32.6 %all_to_all.54.refs_0_ = f32[8,64,1024]{2,1,0:T(8,128)S(1)} all-to-all(f32[8,64,1024]{2,1,0:T(8,128)} %bitcast.30), channel_id=1, replica_groups=mesh['row'=16,'col'=8] {'col'}, dimensions={0} | all-to-all | bytes 4194304 | tf_op jit(solution)/shard_map/all_to_all | solution.py:511
  33.2 3.0 rows_forward.2
  36.3 1.6 all_to_all.35
  37.9 9.4 %all-to-all-start.1 = ((f32[128,34,128]{2,1,0:T(8,128)}), f32[128,34,128]{2,1,0:T(8,128)}, u32[]{:S(2)}, u32[]{:S(2)}) async-start(f32[128,34,128]{2,1,0:T(8,128)} %all_to_all.35), calls=%async_computation.1 | async-start | bytes 5242880 | tf_op jit(solution)/shard_map/all_to_all | solution.py:507
  47.7 8.1 %collective-permute-start = (f32[31,64,128]{2,1,0:T(8,128)S(1)}, f32[31,64,128]{2,1,0:T(8,128)S(1)}, u32[]{:S(2)}, u32[]{:S(2)}) collective-permute-start(f32[31,64,128]{2,1,0:T(8,128)S(1)} %slice.59), channel_id=1, source_target_pairs={{0,127},{1,126},{2,125},{3,124},{4,123},{5,122},{6,121},{7,120},{8... | collective-permute-start | bytes 3047432 | tf_op jit(solution)/shard_map/ppermute | solution.py:552
  56.1 1.5 collective-permute-start.1
  58.3 47.2 %collective-permute-done.m_re = f32[31,64,128]{2,1,0:T(8,128)S(1)} collective-permute-done((f32[31,64,128]{2,1,0:T(8,128)S(1)}, f32[31,64,128]{2,1,0:T(8,128)S(1)}, u32[]{:S(2)}, u32[]{:S(2)}) %collective-permute-start) | collective-permute-done | bytes 1015840 | tf_op jit(solution)/shard_map/ppermute | solution.py:552
  105.6 21.3 %collective-permute-done.1.m_im = f32[31,64,128]{2,1,0:T(8,128)S(1)} collective-permute-done((f32[31,64,128]{2,1,0:T(8,128)S(1)}, f32[31,64,128]{2,1,0:T(8,128)S(1)}, u32[]{:S(2)}, u32[]{:S(2)}) %collective-permute-start.1) | collective-permute-done | bytes 1015840 | tf_op jit(solution)/shard_map/ppermute | solution.py:553
  126.8 9.5 %mirror.1 = (f32[34,64,128]{2,1,0:T(8,128)S(1)}, f32[34,64,128]{2,1,0:T(8,128)S(1)}) custom-call(f32[64,64,128]{2,1,0:T(8,128)S(1)} %bitcast.20, f32[64,64,128]{2,1,0:T(8,128)S(1)} %bitcast.21, f32[31,64,128]{2,1,0:T(8,128)S(1)} %collective-permute-done.m_re, f32[31,64,128]{2,1,0:T(8,128)S(1)} %collective-permute-done.1.m_im, ...), custom_call_target="tpu_custom_call" | custom-call | flops 6000000000 | bytes 4194304 | tf_op jit(solution)/shard_map/mirror/pallas_call | solution.py:384
  138.4 2.5 all_to_all.37.moved
  144.4 15.2 %columns.2 = f32[4352,128]{1,0:T(8,128)S(1)} custom-call(f32[4352,128]{1,0:T(8,128)S(1)} %all_to_all.37.moved, f32[34,64,128]{2,1,0:T(8,128)S(1)} %copy-done.17, f32[34,64,128]{2,1,0:T(8,128)S(1)} %copy-done.20, bf16[2,256,256]{2,1,0:T(8,128)(2,1)S(1)} %copy-done.6, bf16[2,256,256]{2,1,0:T(8,128)(2,1)S(1)} %copy-done.7, bf16[2,256,256]{2,1,0:T(8,128)(2,1)S(1)} %copy-done.8, ...), custom_call_target="tpu_custom_call" | custom-call | flops 8000000000 | bytes 4194304 | tf_op jit(solution)/shard_map/columns/pallas_call | solution.py:384
  159.6 1.4 copy-done.1
  161.0 3.3 all_to_all.38
  164.3 5.1 %all-to-all-start.2 = ((f32[128,34,128]{2,1,0:T(8,128)}), f32[128,34,128]{2,1,0:T(8,128)}, u32[]{:S(2)}, u32[]{:S(2)}) async-start(f32[128,34,128]{2,1,0:T(8,128)} %all_to_all.38), calls=%async_computation.2 | async-start | bytes 5242880 | tf_op jit(solution)/shard_map/all_to_all | solution.py:507
  170.1 34.8 %all-gather = f32[64,512]{1,0:T(8,128)S(1)} all-gather(f32[8,512]{1,0:T(8,128)S(1)} %stack.8), channel_id=2, replica_groups=mesh['row'=16,'col'=8] {'col'}, dimensions={0}, use_global_device_ids=true | all-gather | bytes 147456 | tf_op jit(solution)/shard_map/all_gather | solution.py:528
  205.6 2.4 all_to_all.40.home
  208.1 3.2 rows_inverse.2.r
  214.7 2.2 collective-permute-done.2.edge
  216.9 1.6 copy-done.4
  218.4 18.4 %stations.1 = (f32[8,64,1024]{2,1,0:T(8,128)S(1)}, f32[64,128]{1,0:T(8,128)S(1)}, f32[8,1,512]{2,1,0:T(1,128)S(1)}) custom-call(f32[8,64,1024]{2,1,0:T(8,128)S(1)} %copy-done.4, f32[64,128]{1,0:T(8,128)S(1)} %collective-permute-done.2.edge, f32[8,8,512]{2,1,0:T(8,128)S(1)} %pad_maximum_fusion.st, f32[8,512,8]{2,1,0:T(8,128)S(1)} %bitcast.22), custom_call_target="tpu_custom_call" | custom-call | flops 15000000512 | bytes 4194304 | tf_op jit(solution)/shard_map/stations/pallas_call | solution.py:384
  237.1 6.7 %collective-permute-done.3.refs_1_ = f32[64,128]{1,0:T(8,128)S(1)} collective-permute-done((f32[64,128]{1,0:T(8,128)S(1)}, f32[64,128]{1,0:T(8,128)S(1)}, u32[]{:S(2)}, u32[]{:S(2)}) %collective-permute-start.3) | collective-permute-done | bytes 32800 | tf_op jit(solution)/shard_map/ppermute | solution.py:515
  243.8 3.1 rows_forward.3
  247.0 1.6 all_to_all.41
  248.6 48.9 %all_to_all.55 = f32[128,34,128]{2,1,0:T(8,128)} all-to-all(f32[128,34,128]{2,1,0:T(8,128)} %all_to_all.41), channel_id=1, replica_groups=mesh['row'=16,'col'=8] {'row','col'}, dimensions={0} | all-to-all | bytes 4456448 | tf_op jit(solution)/shard_map/all_to_all | solution.py:507
  297.5 2.4 all_to_all.43.moved
  303.3 15.1 %columns.3 = f32[4352,128]{1,0:T(8,128)S(1)} custom-call(f32[4352,128]{1,0:T(8,128)S(1)} %all_to_all.43.moved, f32[34,64,128]{2,1,0:T(8,128)S(1)} %copy-done.18, f32[34,64,128]{2,1,0:T(8,128)S(1)} %copy-done.21, bf16[2,256,256]{2,1,0:T(8,128)(2,1)S(1)} %copy-done.6, bf16[2,256,256]{2,1,0:T(8,128)(2,1)S(1)} %copy-done.7, bf16[2,256,256]{2,1,0:T(8,128)(2,1)S(1)} %copy-done.8, ...), custom_call_target="tpu_custom_call" | custom-call | flops 8000000000 | bytes 4194304 | tf_op jit(solution)/shard_map/columns/pallas_call | solution.py:384
  319.8 3.3 all_to_all.44
  323.1 41.7 %all_to_all.56 = f32[128,34,128]{2,1,0:T(8,128)} all-to-all(f32[128,34,128]{2,1,0:T(8,128)} %all_to_all.44), channel_id=1, replica_groups=mesh['row'=16,'col'=8] {'row','col'}, dimensions={0} | all-to-all | bytes 4456448 | tf_op jit(solution)/shard_map/all_to_all | solution.py:507
  364.8 2.4 all_to_all.46.home
  367.2 3.2 rows_inverse.3
  371.8 4.7 %all-to-all-start.5 = ((f32[8,64,1024]{2,1,0:T(8,128)}), f32[8,64,1024]{2,1,0:T(8,128)S(1)}, u32[]{:S(2)}, u32[]{:S(2)}) async-start(f32[8,64,1024]{2,1,0:T(8,128)} %copy-done.2), calls=%async_computation.5 | async-start | bytes 4194304 | tf_op jit(solution)/shard_map/all_to_all | solution.py:511
  377.1 39.3 %all-reduce = f32[8,1,512]{2,1,0:T(1,128)S(1)} all-reduce(f32[8,1,512]{2,1,0:T(1,128)S(1)} %get-tuple-element.11), channel_id=3, replica_groups=mesh['row'=16,'col'=8] {'col'}, use_global_device_ids=true, to_apply=%region_0.1.clone | all-reduce | flops 4096 | bytes 32768
  (80 shorter events, 20.5 us)
Async XLA Ops:
  0.6 32.6 %copy-start.6 = (bf16[2,256,256]{2,1,0:T(8,128)(2,1)S(1)}, bf16[2,256,256]{2,1,0:T(8,128)(2,1)}, u32[]{:S(2)}) copy-start(bf16[2,256,256]{2,1,0:T(8,128)(2,1)} %constant.45.clone.refs_1_.tab1.refs_2_) | copy-start | bytes 786436
  0.6 32.6 %copy-start.13 = (f32[2,34,128]{2,1,0:T(8,128)S(1)}, f32[2,34,128]{2,1,0:T(8,128)}, u32[]{:S(2)}) copy-start(f32[2,34,128]{2,1,0:T(8,128)} %constant.46.clone.refs_2_.refs_3_) | copy-start | bytes 104452
  37.9 9.4 %copy-start.22 = (f32[64,8192]{1,0:T(8,128)S(1)}, f32[64,8192]{1,0:T(8,128)}, u32[]{:S(2)}) copy-start(f32[64,8192]{1,0:T(8,128)} %param.18) | copy-start | bytes 6291460
  37.9 100.5 %all-to-all-start.1 = ((f32[128,34,128]{2,1,0:T(8,128)}), f32[128,34,128]{2,1,0:T(8,128)}, u32[]{:S(2)}, u32[]{:S(2)}) async-start(f32[128,34,128]{2,1,0:T(8,128)} %all_to_all.35), calls=%async_computation.1 | async-start | bytes 5242880 | tf_op jit(solution)/shard_map/all_to_all | solution.py:507
  47.4 8.4 %copy-start.23 = (f32[64,8192]{1,0:T(8,128)S(1)}, f32[64,8192]{1,0:T(8,128)}, u32[]{:S(2)}) copy-start(f32[64,8192]{1,0:T(8,128)} %param.19) | copy-start | bytes 6291460
  47.7 57.9 %collective-permute-start = (f32[31,64,128]{2,1,0:T(8,128)S(1)}, f32[31,64,128]{2,1,0:T(8,128)S(1)}, u32[]{:S(2)}, u32[]{:S(2)}) collective-permute-start(f32[31,64,128]{2,1,0:T(8,128)S(1)} %slice.59), channel_id=1, source_target_pairs={{0,127},{1,126},{2,125},{3,124},{4,123},{5,122},{6,121},{7,120},{8... | collective-permute-start | bytes 3047432 | tf_op jit(solution)/shard_map/ppermute | solution.py:552
  56.1 70.7 %collective-permute-start.1 = (f32[31,64,128]{2,1,0:T(8,128)S(1)}, f32[31,64,128]{2,1,0:T(8,128)S(1)}, u32[]{:S(2)}, u32[]{:S(2)}) collective-permute-start(f32[31,64,128]{2,1,0:T(8,128)S(1)} %slice.60), channel_id=1, source_target_pairs={{0,127},{1,126},{2,125},{3,124},{4,123},{5,122},{6,121},{7,120},{8... | collective-permute-start | bytes 3047432 | tf_op jit(solution)/shard_map/ppermute | solution.py:553
  57.9 68.9 %copy-start.14 = (bf16[128,64]{1,0:T(8,128)(2,1)S(1)}, bf16[128,64]{1,0:T(8,128)(2,1)}, u32[]{:S(2)}) copy-start(bf16[128,64]{1,0:T(8,128)(2,1)} %constant.47.clone.rows_tab) | copy-start | bytes 49156
  57.9 68.9 %copy-start.15 = (bf16[128,128]{1,0:T(8,128)(2,1)S(1)}, bf16[128,128]{1,0:T(8,128)(2,1)}, u32[]{:S(2)}) copy-start(bf16[128,128]{1,0:T(8,128)(2,1)} %constant.48.clone.lane_tab) | copy-start | bytes 98308
  138.4 2.5 copy-start.5
  138.4 2.5 copy-start.7
  138.4 2.6 copy-start.8
  138.4 2.6 copy-start.9
  141.9 1.2 copy-start.17
  143.1 1.2 copy-start.20
  159.6 1.4 copy-start.1
  164.2 5.7 %copy-start.26 = (s32[2,512]{1,0:T(2,128)S(1)}, s32[2,512]{1,0:T(2,128)}, u32[]{:S(2)}) copy-start(s32[2,512]{1,0:T(2,128)} %param.20) | copy-start | bytes 12292
  164.2 5.8 %copy-start.25 = (f32[4,512]{1,0:T(4,128)S(1)}, f32[4,512]{1,0:T(4,128)}, u32[]{:S(2)}) copy-start(f32[4,512]{1,0:T(4,128)} %param.21) | copy-start | bytes 24580
  164.3 5.8 %copy-start.27 = (f32[512]{0:T(512)S(1)}, f32[512]{0:T(512)}, u32[]{:S(2)}) copy-start(f32[512]{0:T(512)} %param.22) | copy-start | bytes 6148
  164.3 41.4 %all-to-all-start.2 = ((f32[128,34,128]{2,1,0:T(8,128)}), f32[128,34,128]{2,1,0:T(8,128)}, u32[]{:S(2)}, u32[]{:S(2)}) async-start(f32[128,34,128]{2,1,0:T(8,128)} %all_to_all.38), calls=%async_computation.2 | async-start | bytes 5242880 | tf_op jit(solution)/shard_map/all_to_all | solution.py:507
  205.6 2.5 copy-start.12
  208.1 5.9 %copy-start.24 = (f32[8,5,512]{2,1,0:T(8,128)S(1)}, f32[8,5,512]{2,1,0:T(8,128)}, u32[]{:S(2)}) copy-start(f32[8,5,512]{2,1,0:T(8,128)} %slice.57) | copy-start | bytes 245764
  212.0 1.3 copy-start.3
  213.3 3.6 collective-permute-start.2
  216.9 1.6 copy-start.4
  236.9 6.9 %collective-permute-start.3 = (f32[64,128]{1,0:T(8,128)S(1)}, f32[64,128]{1,0:T(8,128)S(1)}, u32[]{:S(2)}, u32[]{:S(2)}) collective-permute-start(f32[64,128]{1,0:T(8,128)S(1)} %get-tuple-element.10), channel_id=1, source_target_pairs={{0,1},{1,2},{2,3},{3,4},{4,5},{5,6},{6,7},{7,8},{8,9},{9,10},{10,1... | collective-permute-start | bytes 98312 | tf_op jit(solution)/shard_map/ppermute | solution.py:515
  300.8 1.2 copy-start.18
  302.1 1.2 copy-start.21
  318.4 1.4 copy-start
  370.5 1.3 copy-start.2
  371.8 4.7 %copy-start.28 = (u32[128]{0:T(128)S(1)}, u32[128]{0:T(128)}, u32[]{:S(2)}) copy-start(u32[128]{0:T(128)} %constant.60) | copy-start | bytes 1540
  371.8 45.9 %all-to-all-start.5 = ((f32[8,64,1024]{2,1,0:T(8,128)}), f32[8,64,1024]{2,1,0:T(8,128)S(1)}, u32[]{:S(2)}, u32[]{:S(2)}) async-start(f32[8,64,1024]{2,1,0:T(8,128)} %copy-done.2), calls=%async_computation.5 | async-start | bytes 4194304 | tf_op jit(solution)/shard_map/all_to_all | solution.py:511
  (4 other events, 3.8 us)

commit v2 on v1

--- a/solution.py
+++ b/solution.py
@@ -15,8 +15,10 @@
 N = 8192
 LANES = 128
 SHORT = 64
-PAIRS = 17
+PAIRS = 16
 ROWS = 2 * PAIRS
+BLOCKS = 34
+GROUP = 4
 VMEM_LIMIT = 40 * 1024 * 1024
 
 
@@ -216,56 +218,111 @@
 
     lax.fori_loop(0, 8, lines, 0)
     z[33 * 64 :, :] = jnp.zeros((64, 2 * LANES), F32)
-
-    def pair(j, _):
-        data = z[pl.ds(pl.multiple_of(j * 128, 128), 128), :]
-        res = table_times(tab, data, NT)
-        out[pl.ds(2 * j, 128, stride=ROWS), :] = res[:128]
-        out[pl.ds(2 * j + 1, 128, stride=ROWS), :] = res[128:]
-        return 0
-
-    lax.fori_loop(0, PAIRS, pair, 0, unroll=True)
-
-
-def columns_kernel(conj, moved, g_re, g_im, tab1, tab2, tab2i, tab1i, tw, twt, out):
-    def pair(j, _):
+    quotient = lax.broadcasted_iota(jnp.int32, (128, LANES), 0)
+    left = lax.broadcasted_iota(jnp.int32, (128, LANES), 1) < 64
+
+    for first in range(0, PAIRS, GROUP):
+        res = table_times(tab, z[first * 128 : (first + GROUP) * 128, :], NT)
+        for i in range(GROUP):
+            re = res[:128, i * LANES : (i + 1) * LANES]
+            im = res[128:, i * LANES : (i + 1) * LANES]
+            if first + i == 0:
+                extra = table_times(tab, z[32 * 64 :, :], NT)
+                middle = re[64:65]
+                re = jnp.where((quotient >= 64) & left, extra[:128], re)
+                im = jnp.where((quotient >= 64) & left, extra[128:], im)
+                im = jnp.where((quotient == 0) & left, middle, im)
+            out[pl.ds(2 * (first + i), 128, stride=ROWS), :] = re
+            out[pl.ds(2 * (first + i) + 1, 128, stride=ROWS), :] = im
+
+
+def flip_lines(re, im, rows_tab, lane_tab):
+    lane = lax.broadcasted_iota(jnp.int32, (64, LANES), 1)
+    total = None
+    for part in split(jnp.concatenate([re, im], axis=1)):
+        turned = mm(rows_tab[...], part, NN).astype(BF16)
+        turned = jnp.concatenate([turned[:, :LANES], turned[:, LANES:]], axis=0)
+        done = mm(turned, lane_tab[...], NN)
+        total = done if total is None else total + done
+    return (
+        jnp.where(lane == 0, total[64:128], total[:64]),
+        jnp.where(lane == 0, total[192:], total[128:192]),
+    )
+
+
+def columns_kernel(conj, moved, g_re, g_im, v_re, v_im, tab1, tab2, tab2i, tab1i, tw, twt, rows_tab, lane_tab, out):
+    def part(value, i):
+        lanes = slice(i * LANES, (i + 1) * LANES)
+        return value[:128, lanes], value[128:, lanes]
+
+    for first in range(0, PAIRS, GROUP):
+        rows = [pl.ds(2 * (first + i), 128, stride=ROWS) for i in range(GROUP)]
+        rows_im = [pl.ds(2 * (first + i) + 1, 128, stride=ROWS) for i in range(GROUP)]
         data = jnp.concatenate(
-            [moved[pl.ds(2 * j, 128, stride=ROWS), :], moved[pl.ds(2 * j + 1, 128, stride=ROWS), :]], axis=0
+            [jnp.concatenate([moved[rows[i], :], moved[rows_im[i], :]], axis=0) for i in range(GROUP)], axis=1
         )
         y = table_times(tab1, data, NN)
-        re, im = cmul((y[:128], y[128:]), (tw[0], tw[1]))
-        spec = table_times(tab2, jnp.concatenate([re, im], axis=1), NT)
-        gr = g_re[pl.ds(2 * j, 2)].reshape(128, LANES)
-        gi = g_im[pl.ds(2 * j, 2)].reshape(128, LANES)
-        if conj:
-            gi = -gi
-        re, im = cmul((spec[:128], spec[128:]), (gr, gi))
-        w = table_times(tab2i, jnp.concatenate([re, im], axis=0), NN)
-        re, im = cmul((w[:128], w[128:]), (twt[0], twt[1]))
-        res = table_times(tab1i, jnp.concatenate([re, im], axis=1), NT)
-        out[pl.ds(2 * j, 128, stride=ROWS), :] = res[:128]
-        out[pl.ds(2 * j + 1, 128, stride=ROWS), :] = res[128:]
-        return 0
-
-    lax.fori_loop(0, PAIRS, pair, 0, unroll=True)
+        turned = [jnp.concatenate(cmul(part(y, i), (tw[0], tw[1])), axis=1) for i in range(GROUP)]
+        spec = table_times(tab2, jnp.concatenate(turned, axis=0), NT)
+        product = []
+        for i in range(GROUP):
+            j = first + i
+            gr = g_re[2 * j : 2 * j + 2].reshape(128, LANES)
+            gi = g_im[2 * j : 2 * j + 2].reshape(128, LANES)
+            if conj:
+                gi = -gi
+            re, im = part(spec, i)
+            new_re, new_im = cmul((re, im), (gr, gi))
+            if j == 0:
+                back_re, back_im = flip_lines(re[:64], im[:64], rows_tab, lane_tab)
+                vi = -v_im[...] if conj else v_im[...]
+                add_re, add_im = cmul((back_re, -back_im), (v_re[...], vi))
+                none = jnp.zeros((64, LANES), F32)
+                new_re = new_re + jnp.concatenate([add_re, none], axis=0)
+                new_im = new_im + jnp.concatenate([add_im, none], axis=0)
+            product.append(jnp.concatenate([new_re, new_im], axis=0))
+        w = table_times(tab2i, jnp.concatenate(product, axis=1), NN)
+        turned = [jnp.concatenate(cmul(part(w, i), (twt[0], twt[1])), axis=1) for i in range(GROUP)]
+        res = table_times(tab1i, jnp.concatenate(turned, axis=0), NT)
+        for i in range(GROUP):
+            re, im = part(res, i)
+            out[rows[i], :] = re
+            out[rows_im[i], :] = im
 
 
 def rows_inverse_kernel(scale, home, tab, tw, out, v):
-    def pair(j, _):
-        re = home[pl.ds(2 * j, 128, stride=ROWS), :].T
-        im = home[pl.ds(2 * j + 1, 128, stride=ROWS), :].T
-        y = times_table(jnp.concatenate([re, im], axis=1), tab, NT)
+    quotient = lax.broadcasted_iota(jnp.int32, (128, LANES), 0)
+    left = lax.broadcasted_iota(jnp.int32, (128, LANES), 1) < 64
+
+    def finish(y, j):
         re, im = y[:, :LANES], y[:, LANES:]
         for half in range(2):
             p = 2 * j + half
-            c, s = tw[0, pl.ds(p, 1), :] * scale, tw[1, pl.ds(p, 1), :] * scale
+            c, s = tw[0, p : p + 1, :] * scale, tw[1, p : p + 1, :] * scale
             a, b = re[half * 64 : half * 64 + 64], im[half * 64 : half * 64 + 64]
-            rows = pl.ds(pl.multiple_of(j * 128 + half * 64, 64), 64)
-            v[rows, 0:LANES] = a * c - b * s
-            v[rows, LANES : 2 * LANES] = a * s + b * c
-        return 0
-
-    lax.fori_loop(0, PAIRS, pair, 0, unroll=True)
+            v[p * 64 : p * 64 + 64, 0:LANES] = a * c - b * s
+            v[p * 64 : p * 64 + 64, LANES : 2 * LANES] = a * s + b * c
+
+    for first in range(0, PAIRS, GROUP):
+        data = []
+        for i in range(GROUP):
+            j = first + i
+            re = home[pl.ds(2 * j, 128, stride=ROWS), :]
+            im = home[pl.ds(2 * j + 1, 128, stride=ROWS), :]
+            if j == 0:
+                late = (quotient >= 64) & left
+                extra = jnp.concatenate([jnp.where(late, re, 0.0).T, jnp.where(late, im, 0.0).T], axis=1)
+                middle = im[0:1]
+                re = jnp.where(late, jnp.where(quotient == 64, middle, 0.0), re)
+                im = jnp.where(late | ((quotient == 0) & left), 0.0, im)
+            data.append(jnp.concatenate([re.T, im.T], axis=1))
+        if first == 0:
+            data.append(extra)
+        y = times_table(jnp.concatenate(data, axis=0), tab, NT)
+        for i in range(GROUP):
+            finish(y[i * 128 : (i + 1) * 128], first + i)
+        if first == 0:
+            finish(y[GROUP * 128 :], PAIRS)
 
     def lines(t, _):
         x0 = pl.multiple_of(t * 8, 8)
@@ -358,24 +415,30 @@
     lax.fori_loop(0, 8, assemble, 0)
 
 
-def mirror_kernel(t_re, t_im, m_re, m_im, rows_tab, lane_tab, g_re, g_im):
-    lane = lax.broadcasted_iota(jnp.int32, (64, LANES), 1)
-    g_re[0], g_im[0] = t_re[0], t_im[0]
-    g_re[32], g_im[32] = t_re[32], t_im[32]
-    g_re[33], g_im[33] = jnp.zeros((64, LANES), F32), jnp.zeros((64, LANES), F32)
+def mirror_kernel(place, t_re, t_im, m_re, m_im, n_re, n_im, rows_tab, lane_tab, g_re, g_im, v_re, v_im):
+    q = place[0]
+    zero, low = q == 0, q < 64
+
+    def choose(t, m, n):
+        mean, gap = (t[0] + n[...]) * 0.25, (t[0] - n[...]) * 0.25
+        own = jnp.where(zero, mean, jnp.where(low, t[0], t[32]))
+        other = jnp.where(zero, mean, jnp.where(low, n[...], m[0]))
+        return own, other, jnp.where(zero, gap, 0.0)
+
+    own_re, other_re, gap_re = choose(t_re, m_re, n_re)
+    own_im, other_im, gap_im = choose(t_im, m_im, n_im)
+    back_re, back_im = flip_lines(other_re, other_im, rows_tab, lane_tab)
+    g_re[0], g_im[0] = own_re + back_re, own_im - back_im
+    back_re, back_im = flip_lines(gap_re, gap_im, rows_tab, lane_tab)
+    v_re[...], v_im[...] = gap_re + back_re, gap_im - back_im
 
     def one(p, _):
-        both = jnp.concatenate([m_re[31 - p], m_im[31 - p]], axis=1)
-        total = []
-        for part in split(both):
-            flipped = mm(rows_tab[...], part, NN).astype(BF16)
-            total.append([mm(flipped[:, :LANES], lane_tab[...], NN), mm(flipped[:, LANES:], lane_tab[...], NN)])
-        re, im = total[0][0] + total[1][0], total[0][1] + total[1][1]
-        g_re[p] = t_re[p] + jnp.where(lane == 0, re[64:], re[:64])
-        g_im[p] = t_im[p] - jnp.where(lane == 0, im[64:], im[:64])
+        back_re, back_im = flip_lines(m_re[32 - p], m_im[32 - p], rows_tab, lane_tab)
+        g_re[p] = t_re[p] + back_re
+        g_im[p] = t_im[p] - back_im
         return 0
 
-    lax.fori_loop(1, 32, one, 0)
+    lax.fori_loop(1, 32, one, 0, unroll=True)
 
 
 def call(kernel, out_shape, scratch, *args, name, cost=None):
@@ -401,9 +464,20 @@
     return jax.ShapeDtypeStruct(dims, dtype)
 
 
+def flips():
+    b = np.arange(64)
+    rows = np.zeros((128, 64), np.float32)
+    rows[b, 63 - b] = 1.0
+    rows[64 + b, (64 - b) % 64] = 1.0
+    a = np.arange(128)
+    lanes = np.zeros((128, 128), np.float32)
+    lanes[(128 - a) % 128, a] = 1.0
+    return rows.astype(jnp.bfloat16), lanes.astype(jnp.bfloat16)
+
+
 def tables():
     n = np.arange(LANES)
-    p = np.minimum(np.arange(ROWS), 32)
+    p = np.minimum(np.arange(BLOCKS), 32)
     x1 = np.arange(128) % 64
     fwd, inv = complex_table(128, 1, -1.0), complex_table(128, 1, 1.0)
     fwd2, inv2 = complex_table(64, 2, -1.0), complex_table(64, 2, 1.0)
@@ -416,6 +490,8 @@
         "row_inv": twiddle_table(p, n, 1.0),
         "col_fwd": twiddle_table(n, x1, -1.0),
         "col_inv": twiddle_table(x1, n, 1.0),
+        "flip_rows": flips()[0],
+        "flip_lanes": flips()[1],
     }
 
 
@@ -424,27 +500,28 @@
     return call(
         functools.partial(rows_forward_kernel, carry is not None),
         shape(128 * ROWS, LANES),
-        [pltpu.VMEM((ROWS * 64, 2 * LANES), F32)],
+        [pltpu.VMEM((BLOCKS * 64, 2 * LANES), F32)],
         *args,
         name="rows_forward",
         cost=cost(6),
     )
 
 
-def columns(moved, g_re, g_im, conj, tabs):
+def columns(moved, lines, conj, tabs):
     return call(
         functools.partial(columns_kernel, conj),
         shape(128 * ROWS, LANES),
         [],
         moved,
-        g_re,
-        g_im,
+        *lines,
         tabs["fwd"],
         tabs["fwd2"],
         tabs["inv2"],
         tabs["inv"],
         tabs["col_fwd"],
         tabs["col_inv"],
+        tabs["flip_rows"],
+        tabs["flip_lanes"],
         name="columns",
         cost=cost(8),
     )
@@ -454,7 +531,7 @@
     return call(
         functools.partial(rows_inverse_kernel, scale),
         shape(8, 64, 1024),
-        [pltpu.VMEM((ROWS * 64, 2 * LANES), F32)],
+        [pltpu.VMEM((BLOCKS * 64, 2 * LANES), F32)],
         home,
         tabs["inv"],
         tabs["row_inv"],
@@ -477,34 +554,25 @@
     )
 
 
-def mirror(t_re, t_im, m_re, m_im):
-    b = np.arange(64)
-    rows = np.zeros((128, 64), np.float32)
-    rows[b, 63 - b] = 1.0
-    rows[64 + b, (64 - b) % 64] = 1.0
-    a = np.arange(128)
-    lanes = np.zeros((128, 128), np.float32)
-    lanes[(128 - a) % 128, a] = 1.0
-    return call(
+def mirror(place, t_re, t_im, m_re, m_im, n_re, n_im, tabs):
+    vmem = pl.BlockSpec(memory_space=pltpu.VMEM)
+    return pl.pallas_call(
         mirror_kernel,
-        (shape(ROWS, 64, LANES), shape(ROWS, 64, LANES)),
-        [],
-        t_re,
-        t_im,
-        m_re,
-        m_im,
-        jnp.asarray(rows, BF16),
-        jnp.asarray(lanes, BF16),
+        out_shape=(shape(32, 64, LANES), shape(32, 64, LANES), shape(64, LANES), shape(64, LANES)),
+        in_specs=[pl.BlockSpec(memory_space=pltpu.SMEM)] + [vmem] * 8,
+        out_specs=[vmem] * 4,
+        compiler_params=pltpu.CompilerParams(vmem_limit_bytes=VMEM_LIMIT),
+        cost_estimate=cost(6),
         name="mirror",
-        cost=cost(6),
-    )
+    )(place, t_re, t_im, m_re, m_im, n_re, n_im, tabs["flip_rows"], tabs["flip_lanes"])
 
 
 BOTH = ("row", "col")
 
 
 def swap(array):
-    return lax.all_to_all(array, BOTH, split_axis=0, concat_axis=0, tiled=True)
+    pieces = array.reshape(128, ROWS, LANES)
+    return lax.all_to_all(pieces, BOTH, split_axis=0, concat_axis=0, tiled=True).reshape(128 * ROWS, LANES)
 
 
 def across(array):
@@ -549,24 +617,31 @@
     t_re = transfer_real.reshape(64, 64, 128)
     t_im = transfer_imag.reshape(64, 64, 128)
     mirrored = [(i, 127 - i) for i in range(128)]
-    m_re = lax.ppermute(t_re[33:], BOTH, mirrored)
-    m_im = lax.ppermute(t_im[33:], BOTH, mirrored)
+    first_rows = [(i, 128 - i if i > 64 else 0) for i in range(64, 128)]
+    m_re = lax.ppermute(t_re[32:], BOTH, mirrored)
+    m_im = lax.ppermute(t_im[32:], BOTH, mirrored)
+    n_both = lax.ppermute(jnp.stack([t_re[0], t_im[0]]), BOTH, first_rows)
+    place = (lax.axis_index("row") * 8 + lax.axis_index("col")).reshape(1).astype(jnp.int32)
     st = station_fields(station_cells, station_weights, station_means, station_counts)
     stt = jnp.swapaxes(st, 1, 2)
 
     strip = across(roughness.reshape(8, 64, 1024))
-    moved = swap(rows_forward(strip, None, tabs))
-    g_re, g_im = mirror(t_re, t_im, m_re, m_im)
-    home = swap(columns(moved, g_re, g_im, False, tabs))
+    lines_done = rows_forward(strip, None, tabs)
+    lines_done, m_re, m_im, n_both = lax.optimization_barrier((lines_done, m_re, m_im, n_both))
+    moved = swap(lines_done)
+    lines = mirror(place, t_re, t_im, m_re, m_im, n_both[0], n_both[1], tabs)
+    home = swap(columns(moved, lines, False, tabs))
     response = rows_inverse(home, 1.0 / (N * N), tabs)
 
     edge = ring(response[:, 0, :].reshape(64, 128), -1)
     force, spill, misfits = stations(response, edge, st, stt)
     carry = ring(spill, 1)
-    misfit = lax.psum_scatter(misfits, "col", scatter_dimension=0, tiled=True).reshape(512)
+    shares = across(misfits.reshape(8, 4, 128))
 
     moved = swap(rows_forward(force, carry, tabs))
-    home = swap(columns(moved, g_re, g_im, True, tabs))
+    moved, shares = lax.optimization_barrier((moved, shares))
+    misfit = jnp.sum(shares, axis=0).reshape(512)
+    home = swap(columns(moved, lines, True, tabs))
     scale = math.sqrt(N * N / 65536.0) / (N * N)
     gradient = across(rows_inverse(home, scale, tabs)).reshape(512, 1024)
     return (gradient, misfit)

time: 425 us -> 338 us (0.80)
  blocking collectives: 197 us -> 104 us
  Pallas kernels: 70.9 us -> 52 us
  waiting for transfers between devices: 77.4 us -> 96.2 us
  starting transfers between devices: 29.5 us -> 45.7 us
  local copies, waits for them, and re-layouts: 42 us -> 35.5 us
    all_to_all x1 -> x3, waiting for transfers between devices: 0.01 us -> 80.7 us  [across(): return lax.all_to_all(array, 'col', split_axis=0, concat_axis=0, tiled=True)]
    ppermute x2 -> x3, waiting for transfers between devices: 68.5 us -> 0.01 us  [the longest x1 0.01 us: local(): n_both = lax.ppermute(jnp.stack([t_re[0], t_im[0]]), BOTH, first_rows)]
    all_to_all x3 -> x2, blocking collectives: 123 us -> 74.8 us  [swap(): lax.all_to_all(pieces, BOTH, split_axis=0, concat_axis=0, tiled=True)]
    unnamed x1 -> x0, blocking collectives: 39.3 us -> none
    pallas_call x8 -> x7, Pallas kernels: 70.9 us -> 48.1 us  [call(): pl.pallas_call(kernel, out_shape=out_shape, in_specs=[vmem] * len(args),...]
    all_to_all x8 -> x0, local copies, waits for them, and re-layouts: 19.5 us -> none  [swap(): return lax.all_to_all(array, BOTH, split_axis=0, concat_axis=0, tiled=True)]
    all_to_all x1 -> x3, starting transfers between devices: 4.69 us -> 20.1 us  [across(): return lax.all_to_all(array, 'col', split_axis=0, concat_axis=0, tiled=True)]
    unnamed x65 -> x93, local copies, waits for them, and re-layouts: 20.2 us -> 34.8 us
  transfers between devices with their start and end apart: 7 -> 10, of which waited for: 4 -> 5; matrix products, arithmetic and copies ran while one was open for 1% -> 3% of each run, Pallas kernels for 2% -> 4%
where the time goes in v2:
time: 338 us; the launch traced here: 336 us
  blocking collectives  104 us (31%)
  waiting for transfers between devices  96.2 us (28%)
  Pallas kernels  52 us (15%)
  starting transfers between devices  45.7 us (14%)
  local copies, waits for them, and re-layouts  35.5 us (11%)
    all_to_all x3, waiting for transfers between devices, across(): return lax.all_to_all(array, 'col', split_axis=0, concat_axis=0, tiled=True)  80.7 us
    all_to_all x2, blocking collectives, swap(): lax.all_to_all(pieces, BOTH, split_axis=0, concat_axis=0, tiled=True)  74.8 us
    pallas_call x7, Pallas kernels, call(): pl.pallas_call(kernel, out_shape=out_shape, in_specs=[vmem] * len(args),...  48.1 us
    unnamed x93, local copies, waits for them, and re-layouts  34.8 us
    all_gather x1, blocking collectives, station_fields(): gathered = lax.all_gather(fields, 'col', axis=0, tiled=False)  29.1 us
    all_to_all x3, starting transfers between devices, across(): return lax.all_to_all(array, 'col', split_axis=0, concat_axis=0, tiled=True)  20.1 us
    all_to_all x2, starting transfers between devices, swap(): lax.all_to_all(pieces, BOTH, split_axis=0, concat_axis=0, tiled=True)  14.6 us
    all_to_all x2, waiting for transfers between devices, swap(): lax.all_to_all(pieces, BOTH, split_axis=0, concat_axis=0, tiled=True)  13.9 us
  transfers between devices with their start and end apart: 10, of which 5 were waited for; matrix products, arithmetic and copies ran while one was open for 3% of the time, Pallas kernels for 4%

profile of v2, /device:TPU:1, one launch (start us, length us, event | category | flops | bytes accessed | tf_op | source)
XLA Modules:
  0.0 336.3 jit_solution(7905792657392167974)
XLA Ops:
  0.6 6.0 %all-to-all-start = ((f32[8,64,1024]{2,1,0:T(8,128)}), f32[8,64,1024]{2,1,0:T(8,128)S(1)}, u32[]{:S(2)}, u32[]{:S(2)}) async-start(f32[8,64,1024]{2,1,0:T(8,128)} %bitcast.50), calls=%async_computation | async-start | bytes 4194304 | tf_op jit(solution)/shard_map/all_to_all | solution.py:579
  6.6 1.4 slice_bitcast_fusion.1
  9.3 8.6 %collective-permute-start = (f32[32,64,128]{2,1,0:T(8,128)}, f32[32,64,128]{2,1,0:T(8,128)S(1)}, u32[]{:S(2)}, u32[]{:S(2)}) collective-permute-start(f32[32,64,128]{2,1,0:T(8,128)} %bitcast.23), channel_id=1, source_target_pairs={{0,127},{1,126},{2,125},{3,124},{4,123},{5,122},{6,121},{7,120},{8... | collective-permute-start | bytes 3145736 | tf_op jit(solution)/shard_map/ppermute | solution.py:621
  21.1 55.0 %all-to-all-done.refs_0_ = f32[8,64,1024]{2,1,0:T(8,128)S(1)} async-done(((f32[8,64,1024]{2,1,0:T(8,128)}), f32[8,64,1024]{2,1,0:T(8,128)S(1)}, u32[]{:S(2)}, u32[]{:S(2)}) %all-to-all-start) | async-done | bytes 2097184 | tf_op jit(solution)/shard_map/all_to_all | solution.py:579
  76.1 4.6 %rows_forward.2 = f32[4096,128]{1,0:T(8,128)} custom-call(f32[8,64,1024]{2,1,0:T(8,128)S(1)} %all-to-all-done.refs_0_, bf16[2,256,256]{2,1,0:T(8,128)(2,1)S(1)} %copy-done.5, f32[2,34,128]{2,1,0:T(8,128)S(1)} %copy-done.16), custom_call_target="tpu_custom_call" | custom-call | flops 6000000000 | bytes 4194304 | tf_op jit(solution)/shard_map/rows_forward/pallas_call | solution.py:447
  80.7 9.9 %all-to-all-start.1 = ((f32[128,32,128]{2,1,0:T(8,128)}), f32[128,32,128]{2,1,0:T(8,128)S(1)}, u32[]{:S(2)}, u32[]{:S(2)}) async-start(f32[128,32,128]{2,1,0:T(8,128)} %bitcast.3), calls=%async_computation.1 | async-start | bytes 4194304 | tf_op jit(solution)/shard_map/all_to_all | solution.py:575
  90.6 3.5 %copy.28 = f32[8,8,64,128]{3,2,1,0:T(8,128)} copy(f32[8,8,64,128]{3,1,2,0:T(8,128)} %bitcast.46) | data formatting | bytes 4194304
  94.0 1.7 copy.29
  95.8 1.6 copy-done.1
  97.4 1.6 copy-done.2
  100.5 3.9 %mirror.1 = (f32[32,64,128]{2,1,0:T(8,128)S(1)}, f32[32,64,128]{2,1,0:T(8,128)S(1)}, f32[64,128]{1,0:T(8,128)S(1)}, f32[64,128]{1,0:T(8,128)S(1)}) custom-call(s32[1]{0:T(128)} %bitcast.5.place, f32[64,64,128]{2,1,0:T(8,128)S(1)} %bitcast.38, f32[64,64,128]{2,1,0:T(8,128)S(1)} %bitcast.39, f32[32,64,128]{2,1,0:T(8,128)S(1)} %collective-permute-done.m_re, ...), custom_call_target="tpu_custom_call" | custom-call | flops 6000000000 | bytes 4194304 | tf_op jit(solution)/shard_map/mirror/pallas_call | solution.py:559
  107.7 13.3 %all-to-all-done.1 = f32[128,32,128]{2,1,0:T(8,128)S(1)} async-done(((f32[128,32,128]{2,1,0:T(8,128)}), f32[128,32,128]{2,1,0:T(8,128)S(1)}, u32[]{:S(2)}, u32[]{:S(2)}) %all-to-all-start.1) | async-done | bytes 2097184 | tf_op jit(solution)/shard_map/all_to_all | solution.py:575
  130.2 7.1 %columns.2 = f32[4096,128]{1,0:T(8,128)S(1)} custom-call(f32[4096,128]{1,0:T(8,128)S(1)} %bitcast.35, f32[32,64,128]{2,1,0:T(8,128)S(1)} %copy-done.27, f32[32,64,128]{2,1,0:T(8,128)S(1)} %copy-done.30, f32[64,128]{1,0:T(8,128)S(1)} %copy-done.33, f32[64,128]{1,0:T(8,128)S(1)} %copy-done.36, bf16[2,256,256]{2,1,0:T(8,128)(2,1)S(1)} %copy-done.5, ...), custom_call_target="tpu_custom_call" | custom-call | flops 8000000000 | bytes 4194304 | tf_op jit(solution)/shard_map/columns/pallas_call | solution.py:447
  137.3 1.3 copy-done
  138.6 4.7 %all-to-all-start.2 = ((f32[128,32,128]{2,1,0:T(8,128)}), f32[128,32,128]{2,1,0:T(8,128)S(1)}, u32[]{:S(2)}, u32[]{:S(2)}) async-start(f32[128,32,128]{2,1,0:T(8,128)} %bitcast.37), calls=%async_computation.2 | async-start | bytes 4194304 | tf_op jit(solution)/shard_map/all_to_all | solution.py:575
  144.1 29.1 %all-gather = f32[64,512]{1,0:T(8,128)S(1)} all-gather(f32[8,512]{1,0:T(8,128)S(1)} %stack.21), channel_id=2, replica_groups=mesh['row'=16,'col'=8] {'col'}, dimensions={0}, use_global_device_ids=true | all-gather | bytes 147456 | tf_op jit(solution)/shard_map/all_gather | solution.py:596
  173.9 2.8 rows_inverse.2.r
  176.7 1.3 copy-done.3
  179.8 1.6 collective-permute-done.3.edge
  181.4 1.6 copy-done.4
  183.0 19.0 %stations.1 = (f32[8,64,1024]{2,1,0:T(8,128)S(1)}, f32[64,128]{1,0:T(8,128)S(1)}, f32[8,1,512]{2,1,0:T(1,128)}) custom-call(f32[8,64,1024]{2,1,0:T(8,128)S(1)} %copy-done.4, f32[64,128]{1,0:T(8,128)S(1)} %collective-permute-done.3.edge, f32[8,8,512]{2,1,0:T(8,128)S(1)} %pad_maximum_fusion.st, f32[8,512,8]{2,1,0:T(8,128)S(1)} %bitcast.42), custom_call_target="tpu_custom_call" | custom-call | flops 15000000512 | bytes 4194304 | tf_op jit(solution)/shard_map/stations/pallas_call | solution.py:447
  201.9 1.3 copy-done.24
  203.3 9.5 %all-to-all-start.4 = ((f32[8,4,128]{2,1,0:T(4,128)}), f32[8,4,128]{2,1,0:T(4,128)S(1)}, u32[]{:S(2)}, u32[]{:S(2)}) async-start(f32[8,4,128]{2,1,0:T(4,128)} %bitcast.17), calls=%async_computation.4 | async-start | bytes 32768 | tf_op jit(solution)/shard_map/all_to_all | solution.py:579
  212.8 1.6 copy-done.25
  214.3 3.4 %rows_forward.3 = f32[4096,128]{1,0:T(8,128)S(1)} custom-call(f32[8,64,1024]{2,1,0:T(8,128)S(1)} %copy-done.25, f32[64,128]{1,0:T(8,128)S(1)} %collective-permute-done.4.refs_1_, bf16[2,256,256]{2,1,0:T(8,128)(2,1)S(1)} %copy-done.5, f32[2,34,128]{2,1,0:T(8,128)S(1)} %copy-done.17), custom_call_target="tpu_custom_call" | custom-call | flops 6000000000 | bytes 4194304 | tf_op jit(solution)/shard_map/rows_forward/pallas_call | solution.py:447
  217.9 40.2 %all_to_all.35 = f32[128,32,128]{2,1,0:T(8,128)S(1)} all-to-all(f32[128,32,128]{2,1,0:T(8,128)S(1)} %bitcast.43), channel_id=1, replica_groups=mesh['row'=16,'col'=8] {'row','col'}, dimensions={0} | all-to-all | bytes 4194304 | tf_op jit(solution)/shard_map/all_to_all | solution.py:575
  258.1 7.2 %columns.3 = f32[4096,128]{1,0:T(8,128)S(1)} custom-call(f32[4096,128]{1,0:T(8,128)S(1)} %bitcast.40, f32[32,64,128]{2,1,0:T(8,128)S(1)} %copy-done.28, f32[32,64,128]{2,1,0:T(8,128)S(1)} %copy-done.31, f32[64,128]{1,0:T(8,128)S(1)} %copy-done.34, f32[64,128]{1,0:T(8,128)S(1)} %copy-done.37, bf16[2,256,256]{2,1,0:T(8,128)(2,1)S(1)} %copy-done.5, ...), custom_call_target="tpu_custom_call" | custom-call | flops 8000000000 | bytes 4194304 | tf_op jit(solution)/shard_map/columns/pallas_call | solution.py:447
  265.3 34.6 %all_to_all.36 = f32[128,32,128]{2,1,0:T(8,128)S(1)} all-to-all(f32[128,32,128]{2,1,0:T(8,128)S(1)} %bitcast.41), channel_id=1, replica_groups=mesh['row'=16,'col'=8] {'row','col'}, dimensions={0} | all-to-all | bytes 4194304 | tf_op jit(solution)/shard_map/all_to_all | solution.py:575
  299.9 4.1 %rows_inverse.3 = f32[8,64,1024]{2,1,0:T(8,128)} custom-call(f32[4096,128]{1,0:T(8,128)S(1)} %bitcast.44, bf16[2,256,256]{2,1,0:T(8,128)(2,1)S(1)} %copy-done.7, f32[2,34,128]{2,1,0:T(8,128)S(1)} %copy-done.15), custom_call_target="tpu_custom_call" | custom-call | flops 6000000000 | bytes 4194304 | tf_op jit(solution)/shard_map/rows_inverse/pallas_call | solution.py:447
  304.0 4.6 %all-to-all-start.6 = ((f32[8,64,1024]{2,1,0:T(8,128)}), f32[8,64,1024]{2,1,0:T(8,128)S(1)}, u32[]{:S(2)}, u32[]{:S(2)}) async-start(f32[8,64,1024]{2,1,0:T(8,128)} %rows_inverse.3), calls=%async_computation.6 | async-start | bytes 4194304 | tf_op jit(solution)/shard_map/all_to_all | solution.py:579
  309.2 25.8 %all-to-all-done.6 = f32[8,64,1024]{2,1,0:T(8,128)S(1)} async-done(((f32[8,64,1024]{2,1,0:T(8,128)}), f32[8,64,1024]{2,1,0:T(8,128)S(1)}, u32[]{:S(2)}, u32[]{:S(2)}) %all-to-all-start.6) | async-done | bytes 2097184 | tf_op jit(solution)/shard_map/all_to_all | solution.py:579
  335.0 1.3 copy.32
  (107 shorter events, 21.7 us)
Async XLA Ops:
  0.6 75.4 %all-to-all-start = ((f32[8,64,1024]{2,1,0:T(8,128)}), f32[8,64,1024]{2,1,0:T(8,128)S(1)}, u32[]{:S(2)}, u32[]{:S(2)}) async-start(f32[8,64,1024]{2,1,0:T(8,128)} %bitcast.50), calls=%async_computation | async-start | bytes 4194304 | tf_op jit(solution)/shard_map/all_to_all | solution.py:579
  6.6 11.3 %copy-start.38 = (f32[64,8192]{1,0:T(8,128)S(1)}, f32[64,8192]{1,0:T(8,128)}, u32[]{:S(2)}) copy-start(f32[64,8192]{1,0:T(8,128)} %param.19) | copy-start | bytes 6291460
  9.3 9.9 %slice-start = ((f32[64,8192]{1,0:T(8,128)}), f32[1,8192]{1,0:T(1,128)S(1)}, s32[]{:S(2)}) async-start(f32[64,8192]{1,0:T(8,128)} %param.18), calls=%async_computation.7 | async-start | bytes 65536 | tf_op jit(solution)/shard_map/slice | solution.py:623
  9.3 9.9 %slice-start.1 = ((f32[64,8192]{1,0:T(8,128)}), f32[1,8192]{1,0:T(1,128)S(1)}, s32[]{:S(2)}) async-start(f32[64,8192]{1,0:T(8,128)} %param.19), calls=%async_computation.8 | async-start | bytes 65536 | tf_op jit(solution)/shard_map/slice | solution.py:623
  9.3 66.8 %copy-start.5 = (bf16[2,256,256]{2,1,0:T(8,128)(2,1)S(1)}, bf16[2,256,256]{2,1,0:T(8,128)(2,1)}, u32[]{:S(2)}) copy-start(bf16[2,256,256]{2,1,0:T(8,128)(2,1)} %constant.47.clone.refs_1_.tab1.refs_2_) | copy-start | bytes 786436
  9.3 66.8 %copy-start.16 = (f32[2,34,128]{2,1,0:T(8,128)S(1)}, f32[2,34,128]{2,1,0:T(8,128)}, u32[]{:S(2)}) copy-start(f32[2,34,128]{2,1,0:T(8,128)} %constant.48.clone.refs_2_.refs_3_) | copy-start | bytes 104452
  9.3 71.4 %collective-permute-start = (f32[32,64,128]{2,1,0:T(8,128)}, f32[32,64,128]{2,1,0:T(8,128)S(1)}, u32[]{:S(2)}, u32[]{:S(2)}) collective-permute-start(f32[32,64,128]{2,1,0:T(8,128)} %bitcast.23), channel_id=1, source_target_pairs={{0,127},{1,126},{2,125},{3,124},{4,123},{5,122},{6,121},{7,120},{8... | collective-permute-start | bytes 3145736 | tf_op jit(solution)/shard_map/ppermute | solution.py:621
  19.1 61.5 %collective-permute-start.1 = (f32[32,64,128]{2,1,0:T(8,128)}, f32[32,64,128]{2,1,0:T(8,128)}, u32[]{:S(2)}, u32[]{:S(2)}) collective-permute-start(f32[32,64,128]{2,1,0:T(8,128)} %bitcast.25), channel_id=1, source_target_pairs={{0,127},{1,126},{2,125},{3,124},{4,123},{5,122},{6,121},{7,120},{8... | collective-permute-start | bytes 3145736 | tf_op jit(solution)/shard_map/ppermute | solution.py:622
  19.8 60.9 %collective-permute-start.2 = (f32[2,64,128]{2,1,0:T(8,128)}, f32[2,64,128]{2,1,0:T(8,128)S(1)}, u32[]{:S(2)}, u32[]{:S(2)}) collective-permute-start(f32[2,64,128]{2,1,0:T(8,128)} %pad_maximum_fusion.1), channel_id=1, source_target_pairs={{64,0},{65,63},{66,62},{67,61},{68,60},{69,59},{70,58},{71,57},{72... | collective-permute-start | bytes 196616 | tf_op jit(solution)/shard_map/ppermute | solution.py:623
  80.7 40.3 %all-to-all-start.1 = ((f32[128,32,128]{2,1,0:T(8,128)}), f32[128,32,128]{2,1,0:T(8,128)S(1)}, u32[]{:S(2)}, u32[]{:S(2)}) async-start(f32[128,32,128]{2,1,0:T(8,128)} %bitcast.3), calls=%async_computation.1 | async-start | bytes 4194304 | tf_op jit(solution)/shard_map/all_to_all | solution.py:575
  90.6 3.5 %copy-start.39 = (f32[64,8192]{1,0:T(8,128)S(1)}, f32[64,8192]{1,0:T(8,128)}, u32[]{:S(2)}) copy-start(f32[64,8192]{1,0:T(8,128)} %param.19) | copy-start | bytes 6291460
  100.5 20.5 %copy-start.12 = (f32[2,128,128]{2,1,0:T(8,128)S(1)}, f32[2,128,128]{2,1,0:T(8,128)}, u32[]{:S(2)}) copy-start(f32[2,128,128]{2,1,0:T(8,128)} %constant.54.clone.tw) | copy-start | bytes 393220
  138.6 5.4 %copy-start.41 = (s32[2,512]{1,0:T(2,128)S(1)}, s32[2,512]{1,0:T(2,128)}, u32[]{:S(2)}) copy-start(s32[2,512]{1,0:T(2,128)} %param.20) | copy-start | bytes 12292
  138.6 5.4 %copy-start.40 = (f32[4,512]{1,0:T(4,128)S(1)}, f32[4,512]{1,0:T(4,128)}, u32[]{:S(2)}) copy-start(f32[4,512]{1,0:T(4,128)} %param.21) | copy-start | bytes 24580
  138.6 5.4 %copy-start.42 = (f32[512]{0:T(512)S(1)}, f32[512]{0:T(512)}, u32[]{:S(2)}) copy-start(f32[512]{0:T(512)} %param.22) | copy-start | bytes 6148
  138.6 35.3 %copy-start.7 = (bf16[2,256,256]{2,1,0:T(8,128)(2,1)S(1)}, bf16[2,256,256]{2,1,0:T(8,128)(2,1)}, u32[]{:S(2)}) copy-start(bf16[2,256,256]{2,1,0:T(8,128)(2,1)} %constant.53.clone.tab1i.tab) | copy-start | bytes 786436
  138.6 35.3 %copy-start.15 = (f32[2,34,128]{2,1,0:T(8,128)S(1)}, f32[2,34,128]{2,1,0:T(8,128)}, u32[]{:S(2)}) copy-start(f32[2,34,128]{2,1,0:T(8,128)} %constant.56.clone.tw) | copy-start | bytes 104452
  138.6 35.2 %all-to-all-start.2 = ((f32[128,32,128]{2,1,0:T(8,128)}), f32[128,32,128]{2,1,0:T(8,128)S(1)}, u32[]{:S(2)}, u32[]{:S(2)}) async-start(f32[128,32,128]{2,1,0:T(8,128)} %bitcast.37), calls=%async_computation.2 | async-start | bytes 4194304 | tf_op jit(solution)/shard_map/all_to_all | solution.py:575
  178.0 3.3 collective-permute-start.3
  183.0 29.8 %copy-start.17 = (f32[2,34,128]{2,1,0:T(8,128)S(1)}, f32[2,34,128]{2,1,0:T(8,128)}, u32[]{:S(2)}) copy-start(f32[2,34,128]{2,1,0:T(8,128)} %constant.48.clone.refs_2_.refs_3_) | copy-start | bytes 104452
  203.3 9.5 %collective-permute-start.4 = (f32[64,128]{1,0:T(8,128)S(1)}, f32[64,128]{1,0:T(8,128)S(1)}, u32[]{:S(2)}, u32[]{:S(2)}) collective-permute-start(f32[64,128]{1,0:T(8,128)S(1)} %get-tuple-element.24), channel_id=1, source_target_pairs={{0,1},{1,2},{2,3},{3,4},{4,5},{5,6},{6,7},{7,8},{8,9},{9,10},{10,1... | collective-permute-start | bytes 98312 | tf_op jit(solution)/shard_map/ppermute | solution.py:583
  203.3 14.5 %all-to-all-start.4 = ((f32[8,4,128]{2,1,0:T(4,128)}), f32[8,4,128]{2,1,0:T(4,128)S(1)}, u32[]{:S(2)}, u32[]{:S(2)}) async-start(f32[8,4,128]{2,1,0:T(4,128)} %bitcast.17), calls=%async_computation.4 | async-start | bytes 32768 | tf_op jit(solution)/shard_map/all_to_all | solution.py:579
  217.8 40.3 %copy-start.9 = (bf16[2,256,256]{2,1,0:T(8,128)(2,1)S(1)}, bf16[2,256,256]{2,1,0:T(8,128)(2,1)}, u32[]{:S(2)}) copy-start(bf16[2,256,256]{2,1,0:T(8,128)(2,1)} %constant.51.clone.tab2) | copy-start | bytes 786436
  217.8 40.3 %copy-start.11 = (bf16[2,256,256]{2,1,0:T(8,128)(2,1)S(1)}, bf16[2,256,256]{2,1,0:T(8,128)(2,1)}, u32[]{:S(2)}) copy-start(bf16[2,256,256]{2,1,0:T(8,128)(2,1)} %constant.52.clone.tab2i) | copy-start | bytes 786436
  217.8 40.3 %copy-start.14 = (f32[2,128,128]{2,1,0:T(8,128)S(1)}, f32[2,128,128]{2,1,0:T(8,128)}, u32[]{:S(2)}) copy-start(f32[2,128,128]{2,1,0:T(8,128)} %constant.55.clone.twt) | copy-start | bytes 393220
  217.8 40.3 %copy-start.20 = (bf16[128,64]{1,0:T(8,128)(2,1)S(1)}, bf16[128,64]{1,0:T(8,128)(2,1)}, u32[]{:S(2)}) copy-start(bf16[128,64]{1,0:T(8,128)(2,1)} %constant.49.clone.rows_tab) | copy-start | bytes 49156
  217.8 40.3 %copy-start.23 = (bf16[128,128]{1,0:T(8,128)(2,1)S(1)}, bf16[128,128]{1,0:T(8,128)(2,1)}, u32[]{:S(2)}) copy-start(bf16[128,128]{1,0:T(8,128)(2,1)} %constant.50.clone.lane_tab) | copy-start | bytes 98308
  217.8 40.3 %copy-start.28 = (f32[32,64,128]{2,1,0:T(8,128)S(1)}, f32[32,64,128]{2,1,0:T(8,128)}, u32[]{:S(2)}) copy-start(f32[32,64,128]{2,1,0:T(8,128)} %copy-done.26) | copy-start | bytes 3145732
  217.8 40.3 %copy-start.31 = (f32[32,64,128]{2,1,0:T(8,128)S(1)}, f32[32,64,128]{2,1,0:T(8,128)}, u32[]{:S(2)}) copy-start(f32[32,64,128]{2,1,0:T(8,128)} %copy-done.29) | copy-start | bytes 3145732
  217.8 40.3 %copy-start.34 = (f32[64,128]{1,0:T(8,128)S(1)}, f32[64,128]{1,0:T(8,128)}, u32[]{:S(2)}) copy-start(f32[64,128]{1,0:T(8,128)} %copy-done.32) | copy-start | bytes 98308
  217.8 40.3 %copy-start.37 = (f32[64,128]{1,0:T(8,128)S(1)}, f32[64,128]{1,0:T(8,128)}, u32[]{:S(2)}) copy-start(f32[64,128]{1,0:T(8,128)} %copy-done.35) | copy-start | bytes 98308
  304.0 31.0 %all-to-all-start.6 = ((f32[8,64,1024]{2,1,0:T(8,128)}), f32[8,64,1024]{2,1,0:T(8,128)S(1)}, u32[]{:S(2)}, u32[]{:S(2)}) async-start(f32[8,64,1024]{2,1,0:T(8,128)} %rows_inverse.3), calls=%async_computation.6 | async-start | bytes 4194304 | tf_op jit(solution)/shard_map/all_to_all | solution.py:579
  (23 other events, 24.3 us)

commit v3 on v2

--- a/solution.py
+++ b/solution.py
@@ -19,7 +19,8 @@
 ROWS = 2 * PAIRS
 BLOCKS = 34
 GROUP = 4
-VMEM_LIMIT = 40 * 1024 * 1024
+MIB = 1024 * 1024
+VMEM_LIMIT = 40 * MIB
 
 
 def split_np(table):
@@ -189,20 +190,12 @@
     return out
 
 
-def rows_forward_kernel(has_carry, *refs):
-    if has_carry:
-        strip, carry, tab, tw, out, z = refs
-    else:
-        strip, tab, tw, out, z = refs
-
+def rows_forward_kernel(strip, tab, tw, out, z):
     def lines(t, _):
         x0 = pl.multiple_of(t * 8, 8)
         x = []
         for m in range(64):
             value = strip[m // 8, pl.ds(x0, 8), (m % 8) * LANES : (m % 8 + 1) * LANES]
-            if has_carry:
-                here = (lax.broadcasted_iota(jnp.int32, (8, LANES), 0) + x0) == 0
-                value = value + jnp.where(here, carry[m : m + 1, :], 0.0)
             x.append(value)
         done = real_fft64(x)
         for p in range(33):
@@ -250,7 +243,20 @@
     )
 
 
-def columns_kernel(conj, moved, g_re, g_im, v_re, v_im, tab1, tab2, tab2i, tab1i, tw, twt, rows_tab, lane_tab, out):
+def columns_kernel(conj, fetch, moved, *refs):
+    sources, out = refs[:8], refs[8]
+    copies, held = [], sources
+    if fetch:
+        held, sems = refs[9:17], refs[17]
+        copies = [pltpu.make_async_copy(sources[i], held[i], sems.at[i]) for i in range(8)]
+    for copy in copies:
+        copy.start()
+    tab, tws, g_re, g_im, v_re, v_im, rows_tab, lane_tab = held
+    tab1, tab2, tab2i, tab1i = (tab.at[2 * i : 2 * i + 2] for i in range(4))
+    tw, twt = tws.at[0:2], tws.at[2:4]
+    for copy in copies[:1]:
+        copy.wait()
+
     def part(value, i):
         lanes = slice(i * LANES, (i + 1) * LANES)
         return value[:128, lanes], value[128:, lanes]
@@ -262,9 +268,15 @@
             [jnp.concatenate([moved[rows[i], :], moved[rows_im[i], :]], axis=0) for i in range(GROUP)], axis=1
         )
         y = table_times(tab1, data, NN)
+        if first == 0:
+            for copy in copies[1:2]:
+                copy.wait()
         turned = [jnp.concatenate(cmul(part(y, i), (tw[0], tw[1])), axis=1) for i in range(GROUP)]
         spec = table_times(tab2, jnp.concatenate(turned, axis=0), NT)
         product = []
+        if first == 0:
+            for copy in copies[2:]:
+                copy.wait()
         for i in range(GROUP):
             j = first + i
             gr = g_re[2 * j : 2 * j + 2].reshape(128, LANES)
@@ -338,81 +350,183 @@
     lax.fori_loop(0, 8, lines, 0)
 
 
-def stations_kernel(r, edge, st, stt, force, spill, mis_out, r4, f4):
+def bits3(x):
+    hi = x.astype(BF16).astype(F32)
+    mid = (x - hi).astype(BF16).astype(F32)
+    return hi, mid, x - hi - mid
+
+
+def list_kernel(fields, flags, packed, ranks, tri):
+    rows = lax.broadcasted_iota(jnp.int32, (1024, 1024), 0)
+    tri[...] = jnp.where(rows <= lax.broadcasted_iota(jnp.int32, (1024, 1024), 1), 1.0, 0.0).astype(BF16)
+
+    def tile(t, _):
+        flag = flags[t]
+        upto = mm(jnp.broadcast_to(flag, (16, 1024)).astype(BF16), tri[...], NN)[0:1]
+        rank = upto * flag
+        ranks[t] = rank
+        place = jnp.where(rows.astype(F32) + 1.0 == rank, 1.0, 0.0).astype(BF16)
+        values = fields[t]
+        parts = jnp.concatenate([*bits3(values), jnp.zeros((8, 1024), F32)], axis=0).astype(BF16)
+        res = mm(parts, place, NT)
+        packed[t] = res[0:8] + res[8:16] + res[16:24]
+        return 0
+
+    lax.fori_loop(0, 8, tile, 0)
+
+
+def unlist_kernel(packed, ranks, out):
+    rows = lax.broadcasted_iota(jnp.int32, (1024, 512), 0).astype(F32) + 1.0
+
+    def tile(t, _):
+        found = packed[t]
+        line = jnp.concatenate([found[b : b + 1] for b in range(8)], axis=1)
+        parts = jnp.concatenate([*bits3(line), jnp.zeros((13, 1024), F32)], axis=0).astype(BF16)
+        place = jnp.where(rows == ranks[t][:, :512], 1.0, 0.0).astype(BF16)
+        res = mm(parts, place, NN)
+        out[t] = res[0:1] + res[1:2] + res[2:3]
+        return 0
+
+    lax.fori_loop(0, 8, tile, 0)
+
+
+def columns_of(packed, t, b):
+    start = b * 128 if isinstance(b, int) else pl.multiple_of(b * 128, 128)
+    found = packed[t, :, pl.ds(start, 128)]
+    return found, found.T
+
+
+def own_keys(m, line):
+    upper = jnp.where(line >= 2.0, m * 64.0 + line - 2.0, -1.0)
+    lower = jnp.where((line >= 1.0) & (line <= 64.0), m * 64.0 + line - 1.0, -1.0)
+    return upper, lower
+
+
+def edge_keys(m, line):
+    return jnp.where(line == 1.0, 8.0 + m, -1.0), jnp.where(line == 65.0, m, -1.0)
+
+
+def sampled(got, col):
+    left = jnp.concatenate([col[:, 3:4], col[:, 5:6]], axis=0)
+    right = jnp.concatenate([col[:, 4:5], col[:, 6:7]], axis=0)
+    value = left * got[:, :LANES] + right * got[:, LANES:]
+    value = value[:128] + value[128:]
+    here = lax.broadcasted_iota(jnp.int32, (128, LANES), 1).astype(F32) == col[:, 2:3]
+    return jnp.sum(jnp.where(here, value, 0.0), axis=1, keepdims=True)
+
+
+def eye128():
+    rows = lax.broadcasted_iota(jnp.int32, (128, 128), 0)
+    return rows == lax.broadcasted_iota(jnp.int32, (128, 128), 1)
+
+
+def to_row(column):
+    return jnp.sum(jnp.where(eye128(), column, 0.0), axis=0, keepdims=True)
+
+
+def to_column(row):
+    return jnp.sum(jnp.where(eye128(), row, 0.0), axis=1, keepdims=True)
+
+
+def more_blocks(block, blocks):
+    def tile(t, _):
+        def one(b, _):
+            block(t, b)
+            return 0
+
+        lax.fori_loop(1, blocks[t], one, 0)
+        return 0
+
+    lax.fori_loop(0, 8, tile, 0)
+
+
+def sample_kernel(scale, home, tab, tw, packed, blocks, partial, top, bottom, v, out, r2):
+    rows_inverse_kernel(scale, home, tab, tw, out, v)
+    for m in range(64):
+        lanes = slice((m % 8) * LANES, (m % 8 + 1) * LANES)
+        top[m : m + 1, :] = out[m // 8, 0:1, lanes]
+        bottom[m : m + 1, :] = out[m // 8, 63:64, lanes]
     lane64 = lax.broadcasted_iota(jnp.int32, (64, LANES), 1)
-    row64 = lax.broadcasted_iota(jnp.int32, (64, LANES), 0)
-    eye = lax.broadcasted_iota(jnp.int32, (128, 128), 0) == lax.broadcasted_iota(jnp.int32, (128, 128), 1)
-
-    def shifted(t, _):
-        after = lax.rem(t + 1, 8)
-        own, down = [], []
-        for m in range(9):
-            a = r[t, :, m * LANES : (m + 1) * LANES] if m < 8 else r[after, :, 0:LANES]
-            line = edge[pl.ds(t * 8 + m, 1), :] if m < 8 else edge[pl.ds(after * 8, 1), :]
-            own.append(a)
-            down.append(jnp.where(row64 == 63, line, pltpu.roll(a, 63, 0)))
-        own_l = [pltpu.roll(a, LANES - 1, 1) for a in own]
-        down_l = [pltpu.roll(a, LANES - 1, 1) for a in down]
+    key_cols = lax.broadcasted_iota(jnp.int32, (256, 512), 1).astype(F32)
+
+    def block(t, b):
+        _, col = columns_of(packed, t, b)
+        keys = jnp.concatenate(own_keys(col[:, 0:1], col[:, 1:2]), axis=0)
+        pick = jnp.where(key_cols == keys, 1.0, 0.0).astype(BF16)
+        got = mm(pick, r2[t, 0], NN) + mm(pick, r2[t, 1], NN)
+        partial[t, pl.ds(b, 1), :] = to_row(sampled(got, col))
+
+    for t in range(8):
+        after = (t + 1) % 8
+        own = [out[t, :, m * LANES : (m + 1) * LANES] for m in range(8)] + [out[after, :, 0:LANES]]
+        turned = [pltpu.roll(a, LANES - 1, 1) for a in own]
         for m in range(8):
-            rows = pl.ds(pl.multiple_of(t * 512 + m * 64, 64), 64)
-            four = [
-                own[m],
-                jnp.where(lane64 == LANES - 1, own_l[m + 1], own_l[m]),
-                down[m],
-                jnp.where(lane64 == LANES - 1, down_l[m + 1], down_l[m]),
-            ]
-            for k in range(4):
-                hi, lo = split(four[k])
-                r4[0, rows, k * LANES : (k + 1) * LANES] = hi
-                r4[1, rows, k * LANES : (k + 1) * LANES] = lo
-        return 0
-
-    lax.fori_loop(0, 8, shifted, 0)
-
-    lane512 = lax.broadcasted_iota(jnp.int32, (512, LANES), 1).astype(F32)
-    key_cols = lax.broadcasted_iota(jnp.int32, (512, 512), 1).astype(F32)
-    key_rows = lax.broadcasted_iota(jnp.int32, (512, 512), 0).astype(F32)
-
-    def tile(t, _):
-        col = stt[t]
-        key, low = col[:, 0:1], col[:, 1:2]
-        pick = jnp.where(key_cols == key, 1.0, 0.0).astype(BF16)
-        rows = pl.ds(pl.multiple_of(t * 512, 512), 512)
-        got = mm(pick, r4[0, rows, :], NN) + mm(pick, r4[1, rows, :], NN)
-        value = col[:, 2:3] * got[:, 0:LANES]
-        for k in range(1, 4):
-            value = value + col[:, 2 + k : 3 + k] * got[:, k * LANES : (k + 1) * LANES]
-        here = lane512 == low
-        interp = jnp.sum(jnp.where(here, value, 0.0), axis=1, keepdims=True)
-        misfit = jnp.where(col[:, 7:8] > 0.5, interp - col[:, 6:7], 0.0)
-        for i in range(4):
-            part = jnp.where(eye, misfit[i * 128 : (i + 1) * 128], 0.0)
-            mis_out[t, :, i * 128 : (i + 1) * 128] = jnp.sum(part, axis=0, keepdims=True)
-        spread = jnp.where(here, misfit, 0.0)
-        values = jnp.concatenate([spread * col[:, 2 + k : 3 + k] for k in range(4)], axis=1)
+            both = jnp.concatenate([own[m], jnp.where(lane64 == LANES - 1, turned[m + 1], turned[m])], axis=1)
+            hi, lo = split(both)
+            r2[t, 0, m * 64 : m * 64 + 64, :] = hi
+            r2[t, 1, m * 64 : m * 64 + 64, :] = lo
+        block(t, 0)
+
+    more_blocks(block, blocks)
+
+
+def scatter_kernel(packed, partial, blocks, below, above, tab, tw, out, mis, z, strip, f2, edges):
+    lane64 = lax.broadcasted_iota(jnp.int32, (64, LANES), 1)
+    for i, ref in enumerate((below, above)):
+        line = ref[...]
+        turned = pltpu.roll(line, LANES - 1, 1)
+        after = jnp.where(lane64 == LANES - 1, pltpu.roll(turned, 63, 0), turned)
+        for t in range(8):
+            edges[t, i * 8 : i * 8 + 8, 0:LANES] = line[t * 8 : t * 8 + 8]
+            edges[t, i * 8 : i * 8 + 8, LANES:] = after[t * 8 : t * 8 + 8]
+    mis[...] = jnp.zeros((8, 8, 128), F32)
+    edge_cols = lax.broadcasted_iota(jnp.int32, (256, 16), 1).astype(F32)
+    key_rows = lax.broadcasted_iota(jnp.int32, (512, 256), 0).astype(F32)
+    lanes = lax.broadcasted_iota(jnp.int32, (128, LANES), 1).astype(F32)
+
+    def block(t, b):
+        row, col = columns_of(packed, t, b)
+        keys = jnp.concatenate(edge_keys(col[:, 0:1], col[:, 1:2]), axis=0)
+        pick = jnp.where(edge_cols == keys, 1.0, 0.0).astype(BF16)
+        edge_hi, edge_lo = split(edges[t])
+        got = mm(pick, edge_hi, NN) + mm(pick, edge_lo, NN)
+        interp = to_column(partial[t, pl.ds(b, 1), :]) + sampled(got, col)
+        misfit = jnp.where(col[:, 1:2] >= 1.0, interp - col[:, 7:8], 0.0)
+        mis[t, pl.ds(b, 1), :] = to_row(misfit)
+        spread = jnp.where(lanes == col[:, 2:3], misfit, 0.0)
+        values = jnp.concatenate(
+            [
+                jnp.concatenate([spread * col[:, 3:4], spread * col[:, 4:5]], axis=1),
+                jnp.concatenate([spread * col[:, 5:6], spread * col[:, 6:7]], axis=1),
+            ],
+            axis=0,
+        )
         hi, lo = split(values)
-        back = jnp.where(key_rows == st[t, 0:1, :], 1.0, 0.0).astype(BF16)
-        f4[rows, :] = mm(back, hi, NN) + mm(back, lo, NN)
-        return 0
-
-    lax.fori_loop(0, 8, tile, 0)
+        keys = jnp.concatenate(own_keys(row[0:1], row[1:2]), axis=1)
+        back = jnp.where(key_rows == keys, 1.0, 0.0).astype(BF16)
+        return mm(back, hi, NN) + mm(back, lo, NN)
+
+    for t in range(8):
+        f2[t * 512 : t * 512 + 512, :] = block(t, 0)
+
+    def add_block(t, b):
+        f2[pl.ds(pl.multiple_of(t * 512, 512), 512), :] += block(t, b)
+
+    more_blocks(add_block, blocks)
 
     def assemble(t, _):
         before = lax.rem(t + 7, 8)
         last = []
         for m in range(-1, 8):
             start = before * 512 + 448 if m < 0 else t * 512 + m * 64
-            rows = pl.ds(pl.multiple_of(start, 64), 64)
-            last.append([pltpu.roll(f4[rows, k * LANES : (k + 1) * LANES], 1, 1) for k in (1, 3)])
+            last.append(pltpu.roll(f2[pl.ds(pl.multiple_of(start, 64), 64), LANES:], 1, 1))
         for m in range(8):
-            rows = pl.ds(pl.multiple_of(t * 512 + m * 64, 64), 64)
-            same = f4[rows, 0:LANES] + jnp.where(lane64 == 0, last[m][0], last[m + 1][0])
-            below = f4[rows, 2 * LANES : 3 * LANES] + jnp.where(lane64 == 0, last[m][1], last[m + 1][1])
-            spill[pl.ds(t * 8 + m, 1), :] = below[63:64, :]
-            force[t, :, m * LANES : (m + 1) * LANES] = same + jnp.where(row64 == 0, 0.0, pltpu.roll(below, 1, 0))
+            own = f2[pl.ds(pl.multiple_of(t * 512 + m * 64, 64), 64), 0:LANES]
+            strip[t, :, m * LANES : (m + 1) * LANES] = own + jnp.where(lane64 == 0, last[m], last[m + 1])
         return 0
 
     lax.fori_loop(0, 8, assemble, 0)
+    rows_forward_kernel(strip, tab, tw, out, z)
 
 
 def mirror_kernel(place, t_re, t_im, m_re, m_im, n_re, n_im, rows_tab, lane_tab, g_re, g_im, v_re, v_im):
@@ -441,13 +555,13 @@
     lax.fori_loop(1, 32, one, 0, unroll=True)
 
 
-def call(kernel, out_shape, scratch, *args, name, cost=None):
+def call(kernel, out_shape, scratch, *args, name, cost=None, smem=()):
     single = isinstance(out_shape, jax.ShapeDtypeStruct)
     vmem = pl.BlockSpec(memory_space=pltpu.VMEM)
     return pl.pallas_call(
         kernel,
         out_shape=out_shape,
-        in_specs=[vmem] * len(args),
+        in_specs=[pl.BlockSpec(memory_space=pltpu.SMEM) if i in smem else vmem for i in range(len(args))],
         out_specs=vmem if single else [vmem] * len(out_shape),
         scratch_shapes=scratch,
         compiler_params=pltpu.CompilerParams(vmem_limit_bytes=VMEM_LIMIT),
@@ -484,47 +598,42 @@
     return {
         "fwd": split_np(fwd),
         "inv": split_np(inv),
-        "fwd2": split_np(fwd2),
-        "inv2": split_np(inv2),
+        "columns": jnp.asarray(np.concatenate([split_np(t) for t in (fwd, fwd2, inv2, inv)])),
         "row_fwd": twiddle_table(p, n, -1.0),
         "row_inv": twiddle_table(p, n, 1.0),
-        "col_fwd": twiddle_table(n, x1, -1.0),
-        "col_inv": twiddle_table(x1, n, 1.0),
-        "flip_rows": flips()[0],
-        "flip_lanes": flips()[1],
+        "col_turn": jnp.asarray(np.concatenate([twiddle_table(n, x1, -1.0), twiddle_table(x1, n, 1.0)])),
+        "flip_rows": jnp.asarray(flips()[0]),
+        "flip_lanes": jnp.asarray(flips()[1]),
     }
 
 
-def rows_forward(strip, carry, tabs):
-    args = [strip] + ([] if carry is None else [carry]) + [tabs["fwd"], tabs["row_fwd"]]
+def rows_forward(strip, tabs):
     return call(
-        functools.partial(rows_forward_kernel, carry is not None),
+        rows_forward_kernel,
         shape(128 * ROWS, LANES),
         [pltpu.VMEM((BLOCKS * 64, 2 * LANES), F32)],
-        *args,
+        strip,
+        tabs["fwd"],
+        tabs["row_fwd"],
         name="rows_forward",
-        cost=cost(6),
+        cost=cost(4),
     )
 
 
-def columns(moved, lines, conj, tabs):
-    return call(
-        functools.partial(columns_kernel, conj),
-        shape(128 * ROWS, LANES),
-        [],
-        moved,
-        *lines,
-        tabs["fwd"],
-        tabs["fwd2"],
-        tabs["inv2"],
-        tabs["inv"],
-        tabs["col_fwd"],
-        tabs["col_inv"],
-        tabs["flip_rows"],
-        tabs["flip_lanes"],
+def columns(moved, lines, conj, fetch, tabs):
+    vmem, hbm = pl.BlockSpec(memory_space=pltpu.VMEM), pl.BlockSpec(memory_space=pltpu.HBM)
+    rest = (tabs["columns"], tabs["col_turn"], *lines, tabs["flip_rows"], tabs["flip_lanes"])
+    scratch = [pltpu.VMEM(a.shape, a.dtype) for a in rest] + [pltpu.SemaphoreType.DMA((8,))]
+    return pl.pallas_call(
+        functools.partial(columns_kernel, conj, fetch),
+        out_shape=shape(128 * ROWS, LANES),
+        in_specs=[vmem] + [hbm if fetch else vmem] * 8,
+        out_specs=vmem,
+        scratch_shapes=scratch if fetch else [],
+        compiler_params=pltpu.CompilerParams(vmem_limit_bytes=(60 if fetch else 40) * MIB),
+        cost_estimate=cost(7),
         name="columns",
-        cost=cost(8),
-    )
+    )(moved, *rest)
 
 
 def rows_inverse(home, scale, tabs):
@@ -540,17 +649,62 @@
     )
 
 
-def stations(r, edge, st, stt):
+def listed(fields, flags):
     return call(
-        stations_kernel,
-        (shape(8, 64, 1024), shape(64, LANES), shape(8, 1, 512)),
-        [pltpu.VMEM((2, 4096, 512), BF16), pltpu.VMEM((4096, 512), F32)],
-        r,
-        edge,
-        st,
-        stt,
-        name="stations",
-        cost=cost(15),
+        list_kernel,
+        (shape(8, 8, 1024), shape(8, 1, 1024)),
+        [pltpu.VMEM((1024, 1024), BF16)],
+        fields,
+        flags,
+        name="listed",
+        cost=cost(10),
+    )
+
+
+def unlisted(packed, ranks):
+    return call(unlist_kernel, shape(8, 1, 512), [], packed, ranks, name="unlisted", cost=cost(4))
+
+
+def sample(home, packed, blocks, scale, tabs):
+    return call(
+        functools.partial(sample_kernel, scale),
+        (shape(8, 8, 128), shape(64, LANES), shape(64, LANES)),
+        [
+            pltpu.VMEM((BLOCKS * 64, 2 * LANES), F32),
+            pltpu.VMEM((8, 64, 1024), F32),
+            pltpu.VMEM((8, 2, 512, 256), BF16),
+        ],
+        home,
+        tabs["inv"],
+        tabs["row_inv"],
+        packed,
+        blocks,
+        name="sample",
+        cost=cost(8),
+        smem=(4,),
+    )
+
+
+def scatter(packed, partial, blocks, below, above, tabs):
+    return call(
+        scatter_kernel,
+        (shape(128 * ROWS, LANES), shape(8, 8, 128)),
+        [
+            pltpu.VMEM((BLOCKS * 64, 2 * LANES), F32),
+            pltpu.VMEM((8, 64, 1024), F32),
+            pltpu.VMEM((4096, 256), F32),
+            pltpu.VMEM((8, 16, 256), F32),
+        ],
+        packed,
+        partial,
+        blocks,
+        below,
+        above,
+        tabs["fwd"],
+        tabs["row_fwd"],
+        name="scatter",
+        cost=cost(8),
+        smem=(2,),
     )
 
 
@@ -583,7 +737,7 @@
     return lax.ppermute(array, BOTH, [(i, (i + by) % 128) for i in range(128)])
 
 
-def station_fields(cells, weights, means, counts):
+def candidates(cells, weights, means, counts):
     slots = means.shape[0]
     local_x = cells[0] - lax.axis_index("row") * 512
     local_y = cells[1] - lax.axis_index("col") * 1024
@@ -594,14 +748,22 @@
         + [means, live.astype(F32)]
     )
     gathered = lax.all_gather(fields, "col", axis=0, tiled=False)
-    x = gathered[:, 0] - lax.axis_index("col").astype(F32) * 64.0
-    y = gathered[:, 1]
+    rows = lax.axis_size("row")
+    previous = lax.ppermute(gathered, "row", [(i, (i + 1) % rows) for i in range(rows)])
+    column = lax.axis_index("col")
+    start = column.astype(F32) * 64.0
+    upper = jnp.where(column == 0, previous, gathered)
+    line_own = gathered[:, 0] - start
+    line_upper = upper[:, 0] - jnp.where(column == 0, 512.0, start)
+    flag_own = (line_own >= 0.0) & (line_own < 64.0) & (gathered[:, 7] > 0.5)
+    flag_upper = (line_upper == -1.0) & (upper[:, 7] > 0.5)
+    flags = jnp.concatenate([flag_own, flag_upper], axis=1).astype(F32)
+    both = jnp.concatenate([gathered, upper], axis=2)
+    line = jnp.concatenate([line_own, line_upper], axis=1) + 2.0
+    y = both[:, 1]
     high = jnp.floor(y * (1.0 / 128.0))
-    inside = (x >= 0.0) & (x < 64.0)
-    key = jnp.where(inside, high * 64.0 + x, -1.0)
-    live_here = jnp.where(inside, gathered[:, 7], 0.0)
-    rest = [gathered[:, k] for k in range(2, 7)]
-    return jnp.stack([key, y - high * 128.0] + rest + [live_here], axis=1)
+    packed = jnp.stack([high, line, y - high * 128.0] + [both[:, k] for k in range(2, 7)], axis=1)
+    return packed, flags
 
 
 def local(
@@ -622,26 +784,28 @@
     m_im = lax.ppermute(t_im[32:], BOTH, mirrored)
     n_both = lax.ppermute(jnp.stack([t_re[0], t_im[0]]), BOTH, first_rows)
     place = (lax.axis_index("row") * 8 + lax.axis_index("col")).reshape(1).astype(jnp.int32)
-    st = station_fields(station_cells, station_weights, station_means, station_counts)
-    stt = jnp.swapaxes(st, 1, 2)
+    fields, flags = candidates(station_cells, station_weights, station_means, station_counts)
+    blocks = ((jnp.sum(flags, axis=1) + 127.0) * (1.0 / 128.0)).astype(jnp.int32)
 
     strip = across(roughness.reshape(8, 64, 1024))
-    lines_done = rows_forward(strip, None, tabs)
-    lines_done, m_re, m_im, n_both = lax.optimization_barrier((lines_done, m_re, m_im, n_both))
+    lines_done = rows_forward(strip, tabs)
+    lines_done, m_re, m_im, n_both, fields, flags, blocks = lax.optimization_barrier(
+        (lines_done, m_re, m_im, n_both, fields, flags, blocks)
+    )
     moved = swap(lines_done)
     lines = mirror(place, t_re, t_im, m_re, m_im, n_both[0], n_both[1], tabs)
-    home = swap(columns(moved, lines, False, tabs))
-    response = rows_inverse(home, 1.0 / (N * N), tabs)
-
-    edge = ring(response[:, 0, :].reshape(64, 128), -1)
-    force, spill, misfits = stations(response, edge, st, stt)
-    carry = ring(spill, 1)
-    shares = across(misfits.reshape(8, 4, 128))
-
-    moved = swap(rows_forward(force, carry, tabs))
+    packed, ranks = listed(fields, flags.reshape(8, 1, 1024))
+    home = swap(columns(moved, lines, False, True, tabs))
+
+    partial, top, bottom = sample(home, packed, blocks, 1.0 / (N * N), tabs)
+    below, above = ring(top, -1), ring(bottom, 1)
+    lines_done, mis = scatter(packed, partial, blocks, below, above, tabs)
+
+    moved = swap(lines_done)
+    shares = across(unlisted(mis, ranks).reshape(8, 4, 128))
     moved, shares = lax.optimization_barrier((moved, shares))
     misfit = jnp.sum(shares, axis=0).reshape(512)
-    home = swap(columns(moved, lines, True, tabs))
+    home = swap(columns(moved, lines, True, False, tabs))
     scale = math.sqrt(N * N / 65536.0) / (N * N)
     gradient = across(rows_inverse(home, scale, tabs)).reshape(512, 1024)
     return (gradient, misfit)

time: 338 us -> 349 us (1.033); the launches traced: 336 us -> 342 us
  local copies, waits for them, and re-layouts: 35.5 us -> 13.6 us
  blocking collectives: 104 us -> 121 us
  starting transfers between devices: 45.7 us -> 35.2 us
  waiting for transfers between devices: 96.2 us -> 105 us
  Pallas kernels: 52 us -> 59.8 us
  other arithmetic: 1.38 us -> 5.51 us
    all_to_all x3 -> x2, waiting for transfers between devices: 80.7 us -> 25.8 us  [across(): return lax.all_to_all(array, 'col', split_axis=0, concat_axis=0, tiled=True)]
    all_to_all x2, waiting for transfers between devices: 13.9 us -> 41.6 us  [swap(): lax.all_to_all(pieces, BOTH, split_axis=0, concat_axis=0, tiled=True)]
    unnamed x93 -> x59, local copies, waits for them, and re-layouts: 34.8 us -> 12.6 us
    ppermute x1, waiting for transfers between devices: 0.01 us -> 22 us  [local(): m_re = lax.ppermute(t_re[32:], BOTH, mirrored)]
    all_to_all x0 -> x1, blocking collectives: none -> 16.8 us  [across(): return lax.all_to_all(array, 'col', split_axis=0, concat_axis=0, tiled=True)]
    ppermute x1, waiting for transfers between devices: 0.01 us -> 14.1 us  [local(): m_im = lax.ppermute(t_im[32:], BOTH, mirrored)]
    all_to_all x3 -> x2, starting transfers between devices: 20.1 us -> 10.7 us  [across(): return lax.all_to_all(array, 'col', split_axis=0, concat_axis=0, tiled=True)]
    pallas_call x7 -> x8, Pallas kernels: 48.1 us -> 55.9 us  [the longest x6 37.3 us: call(): pl.pallas_call(kernel, out_shape=out_shape, in_specs=[pl.BlockSpec(memory...]
  transfers between devices with their start and end apart: 10 -> 10, of which waited for: 5 -> 7; matrix products, arithmetic and copies ran while one was open for 3% -> 4% of each run, Pallas kernels for 4% -> 5%
where the time goes in v3:
time: 349 us; the launch traced here: 342 us
  blocking collectives  121 us (35%)
  waiting for transfers between devices  105 us (30%)
  Pallas kernels  59.8 us (17%)
  starting transfers between devices  35.2 us (10%)
  local copies, waits for them, and re-layouts  13.6 us (4%)
  other arithmetic  5.51 us (2%)
    all_to_all x2, blocking collectives, swap(): lax.all_to_all(pieces, BOTH, split_axis=0, concat_axis=0, tiled=True)  72.3 us
    all_to_all x2, waiting for transfers between devices, swap(): lax.all_to_all(pieces, BOTH, split_axis=0, concat_axis=0, tiled=True)  41.6 us
    pallas_call x6, Pallas kernels, call(): pl.pallas_call(kernel, out_shape=out_shape, in_specs=[pl.BlockSpec(memory...  37.3 us
    all_gather x1, blocking collectives, candidates(): gathered = lax.all_gather(fields, 'col', axis=0, tiled=False)  32.2 us
    all_to_all x2, waiting for transfers between devices, across(): return lax.all_to_all(array, 'col', split_axis=0, concat_axis=0, tiled=True)  25.8 us
    ppermute x1, waiting for transfers between devices, local(): m_re = lax.ppermute(t_re[32:], BOTH, mirrored)  22 us
    pallas_call x2, Pallas kernels, columns(): pl.pallas_call(functools.partial(columns_kernel, conj, fetch), out_shape=...  18.6 us
    all_to_all x1, blocking collectives, across(): return lax.all_to_all(array, 'col', split_axis=0, concat_axis=0, tiled=True)  16.8 us
  transfers between devices with their start and end apart: 10, of which 7 were waited for; matrix products, arithmetic and copies ran while one was open for 4% of the time, Pallas kernels for 5%

profile of v3, /device:TPU:1, one launch (start us, length us, event | category | flops | bytes accessed | tf_op | source)
XLA Modules:
  0.0 342.1 jit_solution(2849174945555575633)
XLA Ops:
  0.7 6.1 %all-to-all-start = ((f32[8,64,1024]{2,1,0:T(8,128)}), f32[8,64,1024]{2,1,0:T(8,128)S(1)}, u32[]{:S(2)}, u32[]{:S(2)}) async-start(f32[8,64,1024]{2,1,0:T(8,128)} %bitcast.51), calls=%async_computation | async-start | bytes 4194304 | tf_op jit(solution)/shard_map/all_to_all | solution.py:733
  7.4 1.3 collective-permute-start.2
  9.5 32.2 %all-gather = f32[64,512]{1,0:T(8,128)S(1)} all-gather(f32[8,512]{1,0:T(8,128)S(1)} %stack.22), channel_id=2, replica_groups=mesh['row'=16,'col'=8] {'col'}, dimensions={0}, use_global_device_ids=true | all-gather | bytes 147456 | tf_op jit(solution)/shard_map/all_gather | solution.py:750
  42.4 1.6 collective-permute-start.3
  44.0 1.3 slice_bitcast_fusion
  46.5 4.1 %collective-permute-start.1 = (f32[32,64,128]{2,1,0:T(8,128)}, f32[32,64,128]{2,1,0:T(8,128)S(1)}, u32[]{:S(2)}, u32[]{:S(2)}) collective-permute-start(f32[32,64,128]{2,1,0:T(8,128)} %bitcast.25), channel_id=1, source_target_pairs={{0,127},{1,126},{2,125},{3,124},{4,123},{5,122},{6,121},{7,120},{8... | collective-permute-start | bytes 3145736 | tf_op jit(solution)/shard_map/ppermute | solution.py:784
  51.9 3.1 collective-permute-start
  57.7 1.6 fusion
  59.3 3.3 rows_forward.1
  62.6 1.3 copy-done
  63.9 14.1 %collective-permute-done.1.m_im = f32[32,64,128]{2,1,0:T(8,128)S(1)} collective-permute-done((f32[32,64,128]{2,1,0:T(8,128)}, f32[32,64,128]{2,1,0:T(8,128)S(1)}, u32[]{:S(2)}, u32[]{:S(2)}) %collective-permute-start.1) | collective-permute-done | bytes 1048608 | tf_op jit(solution)/shard_map/ppermute | solution.py:784
  78.0 22.0 %collective-permute-done.m_re = f32[32,64,128]{2,1,0:T(8,128)} collective-permute-done((f32[32,64,128]{2,1,0:T(8,128)}, f32[32,64,128]{2,1,0:T(8,128)}, u32[]{:S(2)}, u32[]{:S(2)}) %collective-permute-start) | collective-permute-done | bytes 1048608 | tf_op jit(solution)/shard_map/ppermute | solution.py:783
  100.0 6.6 %all-to-all-start.1 = ((f32[128,32,128]{2,1,0:T(8,128)}), f32[128,32,128]{2,1,0:T(8,128)}, u32[]{:S(2)}, u32[]{:S(2)}) async-start(f32[128,32,128]{2,1,0:T(8,128)} %bitcast.37), calls=%async_computation.1 | async-start | bytes 4194304 | tf_op jit(solution)/shard_map/all_to_all | solution.py:729
  106.6 2.1 copy.27
  109.6 3.9 %mirror.1 = (f32[32,64,128]{2,1,0:T(8,128)S(1)}, f32[32,64,128]{2,1,0:T(8,128)S(1)}, f32[64,128]{1,0:T(8,128)S(1)}, f32[64,128]{1,0:T(8,128)S(1)}) custom-call(s32[1]{0:T(128)} %bitcast.10.place, f32[64,64,128]{2,1,0:T(8,128)S(1)} %bitcast.41, f32[64,64,128]{2,1,0:T(8,128)S(1)} %bitcast.40, f32[32,64,128]{2,1,0:T(8,128)} %collective-permute-done.m_re, ...), custom_call_target="tpu_custom_call" | custom-call | flops 6000000000 | bytes 4194304 | tf_op jit(solution)/shard_map/mirror/pallas_call | solution.py:713
  116.7 19.7 %all-to-all-done.1 = f32[128,32,128]{2,1,0:T(8,128)} async-done(((f32[128,32,128]{2,1,0:T(8,128)}), f32[128,32,128]{2,1,0:T(8,128)}, u32[]{:S(2)}, u32[]{:S(2)}) %all-to-all-start.1) | async-done | bytes 2097184 | tf_op jit(solution)/shard_map/all_to_all | solution.py:729
  136.5 11.5 %columns.2 = f32[4096,128]{1,0:T(8,128)} custom-call(f32[4096,128]{1,0:T(8,128)} %bitcast.9.moved, bf16[8,256,256]{2,1,0:T(8,128)(2,1)} %constant.54.clone.refs_0_, f32[4,128,128]{2,1,0:T(8,128)} %constant.55.clone.refs_1_, f32[32,64,128]{2,1,0:T(8,128)} %copy-done.11, f32[32,64,128]{2,1,0:T(8,128)} %copy-done.13, f32[64,128]{1,0:T(8,128)} %copy-done.15, ...), custom_call_target="tpu_custom_call" | custom-call | flops 7000000000 | bytes 4194304 | tf_op jit(solution)/shard_map/columns/pallas_call | solution.py:627
  147.9 5.0 %all-to-all-start.2 = ((f32[128,32,128]{2,1,0:T(8,128)}), f32[128,32,128]{2,1,0:T(8,128)S(1)}, u32[]{:S(2)}, u32[]{:S(2)}) async-start(f32[128,32,128]{2,1,0:T(8,128)} %bitcast.52), calls=%async_computation.2 | async-start | bytes 4194304 | tf_op jit(solution)/shard_map/all_to_all | solution.py:729
  153.2 8.3 %listed.1 = (f32[8,8,1024]{2,1,0:T(8,128)S(1)}, f32[8,1,1024]{2,1,0:T(1,128)S(1)}) custom-call(f32[8,8,1024]{2,1,0:T(8,128)S(1)} %copy.23.fields, f32[8,1,1024]{2,1,0:T(1,128)S(1)} %reshape.107.flags), custom_call_target="tpu_custom_call" | custom-call | flops 10000000000 | bytes 4194304 | tf_op jit(solution)/shard_map/listed/pallas_call | solution.py:561
  161.5 21.9 %all-to-all-done.2 = f32[128,32,128]{2,1,0:T(8,128)S(1)} async-done(((f32[128,32,128]{2,1,0:T(8,128)}), f32[128,32,128]{2,1,0:T(8,128)S(1)}, u32[]{:S(2)}, u32[]{:S(2)}) %all-to-all-start.2) | async-done | bytes 2097184 | tf_op jit(solution)/shard_map/all_to_all | solution.py:729
  183.4 9.0 %sample.1 = (f32[8,8,128]{2,1,0:T(8,128)S(1)}, f32[64,128]{1,0:T(8,128)S(1)}, f32[64,128]{1,0:T(8,128)S(1)}) custom-call(f32[4096,128]{1,0:T(8,128)S(1)} %bitcast.38, bf16[2,256,256]{2,1,0:T(8,128)(2,1)S(1)} %copy-done.2, f32[2,34,128]{2,1,0:T(8,128)S(1)} %copy-done.5, f32[8,8,1024]{2,1,0:T(8,128)S(1)} %get-tuple-element.24.packed, ...), custom_call_target="tpu_custom_call" | custom-call | flops 8000000000 | bytes 4194304 | tf_op jit(solution)/shard_map/sample/pallas_call | solution.py:561
  192.4 2.6 collective-permute-start.4
  196.3 10.3 %scatter.1 = (f32[4096,128]{1,0:T(8,128)S(1)}, f32[8,8,128]{2,1,0:T(8,128)S(1)}) custom-call(f32[8,8,1024]{2,1,0:T(8,128)S(1)} %get-tuple-element.24.packed, f32[8,8,128]{2,1,0:T(8,128)S(1)} %get-tuple-element.34.partial, s32[8]{0:T(128)S(1)} %multiply_convert_fusion.blocks, f32[64,128]{1,0:T(8,128)S(1)} %collective-permute-done.4.below, ...), custom_call_target="tpu_custom_call" | custom-call | flops 8000000000 | bytes 4194304 | tf_op jit(solution)/shard_map/scatter/pallas_call | solution.py:561
  206.7 2.3 unlisted.1
  208.9 16.8 %all_to_all.35 = f32[8,4,128]{2,1,0:T(4,128)S(1)} all-to-all(f32[8,4,128]{2,1,0:T(4,128)S(1)} %bitcast.45), channel_id=1, replica_groups=mesh['row'=16,'col'=8] {'col'}, dimensions={0} | all-to-all | bytes 32768 | tf_op jit(solution)/shard_map/all_to_all | solution.py:733
  225.8 37.7 %all_to_all.36 = f32[128,32,128]{2,1,0:T(8,128)S(1)} all-to-all(f32[128,32,128]{2,1,0:T(8,128)S(1)} %bitcast.39), channel_id=1, replica_groups=mesh['row'=16,'col'=8] {'row','col'}, dimensions={0} | all-to-all | bytes 4194304 | tf_op jit(solution)/shard_map/all_to_all | solution.py:729
  263.6 7.1 %columns.3 = f32[4096,128]{1,0:T(8,128)S(1)} custom-call(f32[4096,128]{1,0:T(8,128)S(1)} %bitcast.42, bf16[8,256,256]{2,1,0:T(8,128)(2,1)S(1)} %copy-done.1, f32[4,128,128]{2,1,0:T(8,128)S(1)} %copy-done.3, f32[32,64,128]{2,1,0:T(8,128)S(1)} %copy-done.12, f32[32,64,128]{2,1,0:T(8,128)S(1)} %copy-done.14, f32[64,128]{1,0:T(8,128)S(1)} %copy-done.16, ...), custom_call_target="tpu_custom_call" | custom-call | flops 7000000000 | bytes 4194304 | tf_op jit(solution)/shard_map/columns/pallas_call | solution.py:627
  270.8 34.6 %all_to_all.37 = f32[128,32,128]{2,1,0:T(8,128)S(1)} all-to-all(f32[128,32,128]{2,1,0:T(8,128)S(1)} %bitcast.43), channel_id=1, replica_groups=mesh['row'=16,'col'=8] {'row','col'}, dimensions={0} | all-to-all | bytes 4194304 | tf_op jit(solution)/shard_map/all_to_all | solution.py:729
  305.4 4.1 %rows_inverse.1 = f32[8,64,1024]{2,1,0:T(8,128)} custom-call(f32[4096,128]{1,0:T(8,128)S(1)} %bitcast.44, bf16[2,256,256]{2,1,0:T(8,128)(2,1)S(1)} %copy-done.2, f32[2,34,128]{2,1,0:T(8,128)S(1)} %copy-done.5), custom_call_target="tpu_custom_call" | custom-call | flops 6000000000 | bytes 4194304 | tf_op jit(solution)/shard_map/rows_inverse/pallas_call | solution.py:561
  309.5 4.6 %all-to-all-start.6 = ((f32[8,64,1024]{2,1,0:T(8,128)}), f32[8,64,1024]{2,1,0:T(8,128)S(1)}, u32[]{:S(2)}, u32[]{:S(2)}) async-start(f32[8,64,1024]{2,1,0:T(8,128)} %rows_inverse.1), calls=%async_computation.6 | async-start | bytes 4194304 | tf_op jit(solution)/shard_map/all_to_all | solution.py:733
  314.8 25.8 %all-to-all-done.6 = f32[8,64,1024]{2,1,0:T(8,128)S(1)} async-done(((f32[8,64,1024]{2,1,0:T(8,128)}), f32[8,64,1024]{2,1,0:T(8,128)S(1)}, u32[]{:S(2)}, u32[]{:S(2)}) %all-to-all-start.6) | async-done | bytes 2097184 | tf_op jit(solution)/shard_map/all_to_all | solution.py:733
  340.5 1.3 copy.31
  (82 shorter events, 12.8 us)
Async XLA Ops:
  0.6 6.2 %slice-start = ((f32[64,8192]{1,0:T(8,128)}), f32[1,8192]{1,0:T(1,128)S(1)}, s32[]{:S(2)}) async-start(f32[64,8192]{1,0:T(8,128)} %param.17), calls=%async_computation.7 | async-start | bytes 65536 | tf_op jit(solution)/shard_map/slice | solution.py:785
  0.6 6.2 %slice-start.1 = ((f32[64,8192]{1,0:T(8,128)}), f32[1,8192]{1,0:T(1,128)S(1)}, s32[]{:S(2)}) async-start(f32[64,8192]{1,0:T(8,128)} %param.16), calls=%async_computation.8 | async-start | bytes 65536 | tf_op jit(solution)/shard_map/slice | solution.py:785
  0.7 8.8 %copy-start.24 = (s32[2,512]{1,0:T(2,128)S(1)}, s32[2,512]{1,0:T(2,128)}, u32[]{:S(2)}) copy-start(s32[2,512]{1,0:T(2,128)} %param.18) | copy-start | bytes 12292
  0.7 8.8 %copy-start.23 = (f32[4,512]{1,0:T(4,128)S(1)}, f32[4,512]{1,0:T(4,128)}, u32[]{:S(2)}) copy-start(f32[4,512]{1,0:T(4,128)} %param.19) | copy-start | bytes 24580
  0.7 8.8 %copy-start.25 = (f32[512]{0:T(512)S(1)}, f32[512]{0:T(512)}, u32[]{:S(2)}) copy-start(f32[512]{0:T(512)} %param.20) | copy-start | bytes 6148
  0.7 58.6 %all-to-all-start = ((f32[8,64,1024]{2,1,0:T(8,128)}), f32[8,64,1024]{2,1,0:T(8,128)S(1)}, u32[]{:S(2)}, u32[]{:S(2)}) async-start(f32[8,64,1024]{2,1,0:T(8,128)} %bitcast.51), calls=%async_computation | async-start | bytes 4194304 | tf_op jit(solution)/shard_map/all_to_all | solution.py:733
  7.4 56.5 %collective-permute-start.2 = (f32[2,64,128]{2,1,0:T(8,128)}, f32[2,64,128]{2,1,0:T(8,128)S(1)}, u32[]{:S(2)}, u32[]{:S(2)}) collective-permute-start(f32[2,64,128]{2,1,0:T(8,128)} %pad_maximum_fusion), channel_id=1, source_target_pairs={{64,0},{65,63},{66,62},{67,61},{68,60},{69,59},{70,58},{71,57},{72... | collective-permute-start | bytes 196616 | tf_op jit(solution)/shard_map/ppermute | solution.py:785
  42.4 8.2 %copy-start.19 = (f32[64,8192]{1,0:T(8,128)S(1)}, f32[64,8192]{1,0:T(8,128)}, u32[]{:S(2)}) copy-start(f32[64,8192]{1,0:T(8,128)} %param.16) | copy-start | bytes 6291460
  42.4 13.3 %collective-permute-start.3 = (f32[8,8,512]{2,0,1:T(8,128)}, f32[8,8,512]{2,0,1:T(8,128)}, u32[]{:S(2)}, u32[]{:S(2)}) collective-permute-start(f32[8,8,512]{2,0,1:T(8,128)} %copy.20), channel_id=1, source_target_pairs={{0,8},{8,16},{16,24},{24,32},{32,40},{40,48},{48,56},{56,64},{64,7... | collective-permute-start | bytes 393224 | tf_op jit(solution)/shard_map/ppermute | solution.py:752
  46.5 31.5 %collective-permute-start.1 = (f32[32,64,128]{2,1,0:T(8,128)}, f32[32,64,128]{2,1,0:T(8,128)S(1)}, u32[]{:S(2)}, u32[]{:S(2)}) collective-permute-start(f32[32,64,128]{2,1,0:T(8,128)} %bitcast.25), channel_id=1, source_target_pairs={{0,127},{1,126},{2,125},{3,124},{4,123},{5,122},{6,121},{7,120},{8... | collective-permute-start | bytes 3145736 | tf_op jit(solution)/shard_map/ppermute | solution.py:784
  50.7 8.6 %copy-start.4 = (bf16[2,256,256]{2,1,0:T(8,128)(2,1)S(1)}, bf16[2,256,256]{2,1,0:T(8,128)(2,1)}, u32[]{:S(2)}) copy-start(bf16[2,256,256]{2,1,0:T(8,128)(2,1)} %constant.58.clone.tab) | copy-start | bytes 786436
  50.7 8.6 %copy-start.6 = (f32[2,34,128]{2,1,0:T(8,128)S(1)}, f32[2,34,128]{2,1,0:T(8,128)}, u32[]{:S(2)}) copy-start(f32[2,34,128]{2,1,0:T(8,128)} %constant.59.clone.tw) | copy-start | bytes 104452
  51.9 48.1 %collective-permute-start = (f32[32,64,128]{2,1,0:T(8,128)}, f32[32,64,128]{2,1,0:T(8,128)}, u32[]{:S(2)}, u32[]{:S(2)}) collective-permute-start(f32[32,64,128]{2,1,0:T(8,128)} %bitcast.23), channel_id=1, source_target_pairs={{0,127},{1,126},{2,125},{3,124},{4,123},{5,122},{6,121},{7,120},{8... | collective-permute-start | bytes 3145736 | tf_op jit(solution)/shard_map/ppermute | solution.py:783
  62.6 1.3 copy-start
  100.0 36.4 %all-to-all-start.1 = ((f32[128,32,128]{2,1,0:T(8,128)}), f32[128,32,128]{2,1,0:T(8,128)}, u32[]{:S(2)}, u32[]{:S(2)}) async-start(f32[128,32,128]{2,1,0:T(8,128)} %bitcast.37), calls=%async_computation.1 | async-start | bytes 4194304 | tf_op jit(solution)/shard_map/all_to_all | solution.py:729
  106.6 2.2 copy-start.20
  113.5 1.0 copy-start.11
  147.9 5.0 %copy-start.22 = (f32[8,8,1024]{2,0,1:T(8,128)S(1)}, f32[8,8,1024]{2,0,1:T(8,128)}, u32[]{:S(2)}) copy-start(f32[8,8,1024]{2,0,1:T(8,128)} %fusion) | copy-start | bytes 786436
  147.9 35.4 %all-to-all-start.2 = ((f32[128,32,128]{2,1,0:T(8,128)}), f32[128,32,128]{2,1,0:T(8,128)S(1)}, u32[]{:S(2)}, u32[]{:S(2)}) async-start(f32[128,32,128]{2,1,0:T(8,128)} %bitcast.52), calls=%async_computation.2 | async-start | bytes 4194304 | tf_op jit(solution)/shard_map/all_to_all | solution.py:729
  153.2 30.2 %copy-start.2 = (bf16[2,256,256]{2,1,0:T(8,128)(2,1)S(1)}, bf16[2,256,256]{2,1,0:T(8,128)(2,1)}, u32[]{:S(2)}) copy-start(bf16[2,256,256]{2,1,0:T(8,128)(2,1)} %constant.60.clone.tab) | copy-start | bytes 786436
  153.2 30.2 %copy-start.5 = (f32[2,34,128]{2,1,0:T(8,128)S(1)}, f32[2,34,128]{2,1,0:T(8,128)}, u32[]{:S(2)}) copy-start(f32[2,34,128]{2,1,0:T(8,128)} %constant.61.clone.tw) | copy-start | bytes 104452
  192.4 3.4 %collective-permute-start.4 = (f32[64,128]{1,0:T(8,128)S(1)}, f32[64,128]{1,0:T(8,128)S(1)}, u32[]{:S(2)}, u32[]{:S(2)}) collective-permute-start(f32[64,128]{1,0:T(8,128)S(1)} %get-tuple-element.35), channel_id=1, source_target_pairs={{0,127},{1,0},{2,1},{3,2},{4,3},{5,4},{6,5},{7,6},{8,7},{9,8},{10,... | collective-permute-start | bytes 98312 | tf_op jit(solution)/shard_map/ppermute | solution.py:737
  194.9 1.4 collective-permute-start.5
  225.8 37.8 %copy-start.1 = (bf16[8,256,256]{2,1,0:T(8,128)(2,1)S(1)}, bf16[8,256,256]{2,1,0:T(8,128)(2,1)}, u32[]{:S(2)}) copy-start(bf16[8,256,256]{2,1,0:T(8,128)(2,1)} %constant.54.clone.refs_0_) | copy-start | bytes 3145732
  225.8 37.8 %copy-start.3 = (f32[4,128,128]{2,1,0:T(8,128)S(1)}, f32[4,128,128]{2,1,0:T(8,128)}, u32[]{:S(2)}) copy-start(f32[4,128,128]{2,1,0:T(8,128)} %constant.55.clone.refs_1_) | copy-start | bytes 786436
  225.8 37.8 %copy-start.8 = (bf16[128,128]{1,0:T(8,128)(2,1)S(1)}, bf16[128,128]{1,0:T(8,128)(2,1)}, u32[]{:S(2)}) copy-start(bf16[128,128]{1,0:T(8,128)(2,1)} %constant.57.clone.lane_tab.refs_7_) | copy-start | bytes 98308
  225.8 37.8 %copy-start.10 = (bf16[128,64]{1,0:T(8,128)(2,1)S(1)}, bf16[128,64]{1,0:T(8,128)(2,1)}, u32[]{:S(2)}) copy-start(bf16[128,64]{1,0:T(8,128)(2,1)} %constant.56.clone.rows_tab.refs_6_) | copy-start | bytes 49156
  225.8 37.8 %copy-start.12 = (f32[32,64,128]{2,1,0:T(8,128)S(1)}, f32[32,64,128]{2,1,0:T(8,128)}, u32[]{:S(2)}) copy-start(f32[32,64,128]{2,1,0:T(8,128)} %copy-done.11) | copy-start | bytes 3145732
  225.8 37.8 %copy-start.14 = (f32[32,64,128]{2,1,0:T(8,128)S(1)}, f32[32,64,128]{2,1,0:T(8,128)}, u32[]{:S(2)}) copy-start(f32[32,64,128]{2,1,0:T(8,128)} %copy-done.13) | copy-start | bytes 3145732
  225.8 37.8 %copy-start.16 = (f32[64,128]{1,0:T(8,128)S(1)}, f32[64,128]{1,0:T(8,128)}, u32[]{:S(2)}) copy-start(f32[64,128]{1,0:T(8,128)} %copy-done.15) | copy-start | bytes 98308
  225.8 37.8 %copy-start.18 = (f32[64,128]{1,0:T(8,128)S(1)}, f32[64,128]{1,0:T(8,128)}, u32[]{:S(2)}) copy-start(f32[64,128]{1,0:T(8,128)} %copy-done.17) | copy-start | bytes 98308
  309.5 31.0 %all-to-all-start.6 = ((f32[8,64,1024]{2,1,0:T(8,128)}), f32[8,64,1024]{2,1,0:T(8,128)S(1)}, u32[]{:S(2)}, u32[]{:S(2)}) async-start(f32[8,64,1024]{2,1,0:T(8,128)} %rows_inverse.1), calls=%async_computation.6 | async-start | bytes 4194304 | tf_op jit(solution)/shard_map/all_to_all | solution.py:733
  (6 other events, 4.5 us)
